TPU v7x, 256 devices: a whole 4x4x8 slice. The times are simulated.
256 devices in a mesh: item: 64 (over z, x, core), user: 4 (over y).
Axes of the slice: x: 4, y: 4, z: 8, core: 2. Of those that a mesh axis runs over, the one named last changes fastest.
Arguments:
- basis: float32 [32768, 128], P('item'), may hold values from -8 to 8
- old_values: float32 [128], replicated, may hold values from 0.5 to 2
- ratings: bfloat16 [256, 64, 128], P(('item', 'user')), may hold values from -16 to 16
- block_ids: int32 [256, 64], replicated, may hold values from 0 to 255, as said below
- user_row: int32 [256], replicated, may hold values from 0 to 255, as said below
Outputs:
- new_basis: float32 [32768, 128], P('item')
- user_factors: float32 [256, 128], replicated
Inputs may be any that keep to these rules, and one draw needn't show every extreme that they name: `block_ids`: block g holds items g * 128 to g * 128 + 127; the 64 blocks of one user are distinct; at most 4 of one user's blocks lie in one slab of 512 items (items i * 512 to (i + 1) * 512 - 1), and every user has exactly 4 in some slab. A permutation: user j's tiles are row user_row[j] of ratings.
All inputs are finite; a program needn't handle non-finite values.
Results may differ from a plain program's by a relative error of at most 0.0003.
Values may be sent and summed in bfloat16 or wider, within the bound.
No kernel may reach another device: no remote copies, remote signals or barrier semaphores. Data moves between devices by JAX's collectives and lax.ppermute only.
A program may use at most 128 MiB of HBM per device.

v0:
```python
import functools

import jax
import jax.numpy as jnp
from jax import lax
from jax.experimental import pallas as pl
from jax.experimental.pallas import tpu as pltpu
from jax.sharding import Mesh
from jax.sharding import PartitionSpec as P

ITEM = ("item_0", "item_1", "item_2")
ITEM_USER = ("item_0", "item_1", "item_2", "user")

f32 = jnp.float32
exact_mode = lax.Precision.HIGHEST
RANK, USERS, ORDER = 128, 256, 384


def mm(a, b):
    return jnp.dot(a, b, precision=exact_mode, preferred_element_type=f32)


def mm_nt(a, b):
    return lax.dot_general(a, b, (((1,), (1,)), ((), ())), precision=exact_mode, preferred_element_type=f32)


def spread(x):
    return jnp.broadcast_to(x, (8, RANK))


def eliminate(gram):
    lane = lax.broadcasted_iota(jnp.int32, (8, RANK), 1)
    sub = lax.broadcasted_iota(jnp.int32, (8, RANK), 0)
    count = RANK // 8
    rows = [gram[8 * k : 8 * k + 8, :] for k in range(count)]
    pivots = []
    for panel in range(count):
        here = rows[panel]
        first = 8 * panel
        column = [spread(here[:, first + k : first + k + 1]) for k in range(8)]
        pivot_of_row = jnp.ones((8, RANK), f32)
        kept, inverses, uppers = [], [], []
        for s in range(8):
            upper = [spread(column[k][s : s + 1, :]) for k in range(s, 8)]
            inverse = 1.0 / upper[0]
            line = spread(here[s : s + 1, :])
            pivot_of_row = jnp.where(sub == s, upper[0], pivot_of_row)
            line = jnp.where(lane == first + s, line + line, line)
            kept.append(line)
            inverses.append(inverse)
            uppers.append(upper)
            factor = jnp.where(sub > s, column[s] * inverse, 0.0)
            here = here - factor * line
            for k in range(s + 1, 8):
                column[k] = column[k] - factor * upper[k - s]
        rows[panel] = here
        pivots.append(pivot_of_row)
        for other in range(panel + 1, count):
            there = rows[other]
            column = [spread(there[:, first + k : first + k + 1]) for k in range(8)]
            for s in range(8):
                factor = column[s] * inverses[s]
                there = there - factor * kept[s]
                for k in range(s + 1, 8):
                    column[k] = column[k] - factor * uppers[s][k - s]
            rows[other] = there
    return lower_of(jnp.concatenate(rows, axis=0)), jnp.concatenate(pivots, axis=0)


def square_iotas():
    i = lax.broadcasted_iota(jnp.int32, (RANK, RANK), 0)
    k = lax.broadcasted_iota(jnp.int32, (RANK, RANK), 1)
    return i, k


def lower_of(x):
    i, k = square_iotas()
    return jnp.where(i >= k, x, 0.0)


def eliminate_slowly(gram):
    i, k = square_iotas()

    def step(j, carry):
        x, pivots = carry
        line = jnp.sum(jnp.where(i == j, x, 0.0), axis=0, keepdims=True)
        column = jnp.sum(jnp.where(k == j, x, 0.0), axis=1, keepdims=True)
        pivot = jnp.sum(jnp.where((i == j) & (k == j), x, 0.0), axis=(0, 1), keepdims=True)
        pivots = jnp.where(i == j, pivot, pivots)
        doubled = jnp.where(k[:1] == j, line + line, line)
        x = x - jnp.where(i > j, column / pivot, 0.0) * doubled
        return x, pivots

    x, pivots = lax.fori_loop(0, RANK, step, (gram, jnp.ones((RANK, RANK), f32)))
    return lower_of(x), pivots


def scaled(x, pivots, power):
    factor = 1.0 / pivots if power == 1 else lax.rsqrt(pivots)
    return jnp.concatenate([x[:, c : c + RANK] * factor for c in range(0, x.shape[1], RANK)], axis=1)


def turned(lower, pivots, x):
    return scaled(mm(lower, scaled(x, pivots, 1)), pivots, 2)


def smallest(pivots, gram):
    i, k = square_iotas()
    start = jnp.sum(jnp.where(i == k, gram, 0.0), axis=1, keepdims=True)
    return jnp.min(pivots / start)


def polished(x, y):
    i, k = square_iotas()
    off = mm_nt(x, y) - jnp.where(i == k, 1.0, 0.0)
    step = jnp.where(i > k, off, jnp.where(i == k, 0.5 * off, 0.0))
    return x - mm(step, x), y - mm(step, y)


def assemble(sums, weights, items):
    i, k = square_iotas()
    block = lambda n: sums[RANK * n : RANK * (n + 1), :] * (1.0 / items)
    own = jnp.transpose(block(0) * weights) * weights
    left1, left2 = block(1) * weights, block(2) * weights
    c11, c12, c22 = block(3), block(4), block(5)
    diagonal = jnp.where(i == k, own + c11 + c22, 0.0)
    size = jnp.sum(diagonal, axis=(0, 1), keepdims=True)
    whole = jnp.concatenate(
        [
            jnp.concatenate([own, jnp.transpose(left1), jnp.transpose(left2)], axis=1),
            jnp.concatenate([left1, c11, c12], axis=1),
            jnp.concatenate([left2, jnp.transpose(c12), c22], axis=1),
        ],
        axis=0,
    )
    return whole * (1.0 / size), size


def core_kernel(items, sums_ref, weights_ref, turn_ref, left_ref, factors_ref, gram_ref, turn_t_ref, back_ref):
    weights = weights_ref[...]
    whole, size = assemble(sums_ref, weights, items)
    gram_ref[...] = whole
    g = gram_ref[...]

    x = g[:RANK, :]
    h1 = mm_nt(x, x)
    low1, piv1 = eliminate(h1)
    x = turned(low1, piv1, x)
    x = mm(x, g)
    y = mm(x, g)
    h2 = mm_nt(x, y)
    low2, piv2 = eliminate(h2)
    x = turned(low2, piv2, y)
    x = mm(x, g)
    y = mm(x, g)
    h3 = mm_nt(x, y)
    low3, piv3 = eliminate(h3)
    turn_t_ref[...] = turned(low3, piv3, x)
    back_ref[...] = turned(low3, piv3, y)
    fine = (smallest(piv1, h1) > 1e-4) & (smallest(piv2, h2) > 3e-4) & (smallest(piv3, h3) > 8e-3)

    @pl.when(jnp.logical_not(fine))
    def _():
        def ortho(x, y):
            gram = mm_nt(x, y)
            return eliminate_slowly(gram)

        def sweep(n, x):
            y = mm(x, gram_ref[...])
            low, piv = ortho(x, y)
            y = turned(low, piv, y)
            low, piv = ortho(y, y)
            return turned(low, piv, y)

        start = jnp.where(
            lax.broadcasted_iota(jnp.int32, (RANK, ORDER), 0) == lax.broadcasted_iota(jnp.int32, (RANK, ORDER), 1), 1.0, 0.0
        )
        x = lax.fori_loop(0, 4, sweep, start)
        y = mm(x, gram_ref[...])
        low, piv = ortho(x, y)
        x, y = turned(low, piv, x), turned(low, piv, y)
        x, y = polished(x, y)
        x, y = polished(x, y)
        turn_t_ref[...] = x
        back_ref[...] = y

    scale = lax.rsqrt(size)
    x = turn_t_ref[...] * scale
    left_ref[:, :RANK] = x[:, :RANK] * weights
    left_ref[:, RANK:] = x[:, RANK:]
    user_of = turn_ref[...]
    onehot = jnp.where(lax.broadcasted_iota(jnp.int32, (USERS, USERS), 1) == user_of, 1.0, 0.0)
    factors_ref[...] = mm_nt(onehot, back_ref[:, RANK:] * (scale * size))


def core(sums, weights, user_row, items):
    return pl.pallas_call(
        functools.partial(core_kernel, items),
        out_shape=[jax.ShapeDtypeStruct((RANK, ORDER), f32), jax.ShapeDtypeStruct((USERS, RANK), f32)],
        scratch_shapes=[pltpu.VMEM((ORDER, ORDER), f32), pltpu.VMEM((RANK, ORDER), f32), pltpu.VMEM((RANK, ORDER), f32)],
        compiler_params=pltpu.CompilerParams(vmem_limit_bytes=32 * 2**20),
    )(sums, weights.reshape(1, RANK), user_row.reshape(USERS, 1))


def column_kernel(row_ref, user_row_ref, blocks_ref, tiles_ref, out_ref):
    mine = user_row_ref[...] == row_ref[0]
    blocks = jnp.sum(jnp.where(mine, blocks_ref[...], 0), axis=1, keepdims=True)
    count = out_ref.shape[0]
    place = lax.broadcasted_iota(jnp.int32, (blocks.shape[0], count), 1) == blocks
    place = jnp.where(place, 1.0, 0.0).astype(jnp.bfloat16)
    dense = lax.dot_general(place, tiles_ref[...], (((0,), (0,)), ((), ())), preferred_element_type=f32)
    out_ref[...] = dense.astype(jnp.bfloat16)


def column_of(row, user_row, block_ids, tiles, count):
    in_vmem = pl.BlockSpec(memory_space=pltpu.VMEM)
    return pl.pallas_call(
        column_kernel,
        out_shape=jax.ShapeDtypeStruct((count, tiles.shape[1]), jnp.bfloat16),
        in_specs=[pl.BlockSpec(memory_space=pltpu.SMEM), in_vmem, in_vmem, in_vmem],
        out_specs=in_vmem,
    )(row.reshape(1), user_row.reshape(1, -1), block_ids.T, tiles)


def gram_kernel(basis_ref, slab_ref, out_ref):
    width = slab_ref.shape[2]
    own = left = cross = 0.0
    for b in range(slab_ref.shape[0]):
        rows = basis_ref[width * b : width * (b + 1), :]
        x = slab_ref[b]
        own = own + lax.dot_general(rows, rows, (((0,), (0,)), ((), ())), precision=exact_mode, preferred_element_type=f32)
        left = left + mm(x.astype(f32), rows)
        cross = cross + lax.dot_general(x, x, (((1,), (1,)), ((), ())), preferred_element_type=f32)
    out_ref[0:128, :] = own
    out_ref[128:384, :] = left
    out_ref[384:512, :] = cross[:128, :128]
    out_ref[512:640, :] = cross[:128, 128:]
    out_ref[640:768, :] = cross[128:, 128:]


def gram_parts(basis, slab):
    return pl.pallas_call(gram_kernel, out_shape=jax.ShapeDtypeStruct((768, RANK), f32))(basis, slab)


def rows_kernel(basis_ref, slab_ref, left_ref, out_ref):
    width = slab_ref.shape[2]
    for b in range(slab_ref.shape[0]):
        here = slice(width * b, width * (b + 1))
        x = jnp.transpose(slab_ref[b].astype(f32))
        out_ref[here, :] = mm_nt(basis_ref[here, :], left_ref[:, :RANK]) + mm_nt(x, left_ref[:, RANK:])


def new_rows(basis, slab, left):
    return pl.pallas_call(rows_kernel, out_shape=jax.ShapeDtypeStruct(basis.shape, f32))(basis, slab, left)


def copies(x, axis):
    x = jnp.broadcast_to(x, (lax.axis_size(axis), *x.shape))
    return lax.all_to_all(x, axis, split_axis=0, concat_axis=0, tiled=True)


def summed(parts):
    far = ("item_0", "item_1")
    pieces = parts.reshape(2, lax.axis_size(far), -1, RANK)
    near = lax.all_to_all(pieces, "item_2", 0, 0, tiled=True).sum(axis=0)
    own = lax.all_to_all(near, far, 0, 0, tiled=True).sum(axis=0)
    half = copies(own, far)
    return copies(half, "item_2").reshape(parts.shape)


def per_device(basis, old_values, ratings, block_ids, user_row):
    n_item = lax.axis_size(ITEM)
    n_user = lax.axis_size("user")
    width = ratings.shape[2]
    slab_blocks = basis.shape[0] // width
    row = lax.axis_index(ITEM) * n_user + lax.axis_index("user")
    column = column_of(row, user_row, block_ids, ratings[0], n_item * slab_blocks)
    arrived = lax.all_to_all(column.reshape(n_item, slab_blocks, width), ITEM, 0, 0, tiled=True)
    pooled = copies(arrived, "user")
    slab = pooled.reshape(USERS, slab_blocks, width).swapaxes(0, 1)
    sums = summed(gram_parts(basis, slab))
    place = user_row % n_user * n_item + user_row // n_user
    left, user_factors = core(sums, old_values, place, basis.shape[0] * n_item)
    return new_rows(basis, slab, left), user_factors


def solution(mesh):
    finer = Mesh(
        mesh.devices.reshape(8, 4, 2, mesh.shape["user"]), ("item_0", "item_1", "item_2", "user")
    )
    placed = (P(ITEM, None), P(), P(ITEM_USER, None, None), P(), P())
    return jax.shard_map(
        per_device, mesh=finer, in_specs=placed, out_specs=(P(ITEM, None), P()), check_vma=False
    )
```

profile of v0, /device:TPU:1, one launch (start us, length us, event | category | flops | bytes accessed | tf_op | source)
XLA Modules:
  0.0 106.0 jit_solution(15316715384505145961)
XLA Ops:
  0.6 1.8 %shard_map.68 = bf16[256,128]{1,0:T(8,128)(2,1)} custom-call(s32[1]{0:T(128)} %bitcast.row_ref, s32[1,256]{1,0:T(1,128)} %bitcast.16, s32[64,256]{1,0:T(8,128)} %bitcast.14, bf16[64,128]{1,0:T(8,128)(2,1)} %bitcast.15), custom_call_target="tpu_custom_call" | custom-call | tf_op jit(solution)/shard_map/pallas_call | solution.py:217
  2.4 23.1 %all_to_all.30 = bf16[64,4,128]{2,1,0:T(4,128)(2,1)S(1)} all-to-all(bf16[64,4,128]{2,1,0:T(4,128)(2,1)} %bitcast.13), channel_id=1, replica_groups=mesh['item_0'=8,'item_1'=4,'item_2'=2,'user'=4] {'item_0','item_1','item..., dimensions={0} | all-to-all | bytes 131072 | tf_op jit(solution)/shard_map/all_to_all | solution.py:278
  25.5 9.8 %all_to_all.31 = bf16[4,64,4,128]{3,1,2,0:T(8,128)(2,1)S(1)} all-to-all(bf16[4,64,4,128]{3,1,2,0:T(8,128)(2,1)S(1)} %broadcast_in_dim.9), channel_id=1, replica_groups=mesh['item_0'=8,'item_1'=4,'item_2'=2,'user'=4] {'user'}, dimensions={0} | all-to-all | bytes 524288 | tf_op jit(solution)/shard_map/all_to_all | solution.py:259
  35.3 0.7 copy.22
  36.0 2.7 %shard_map.69 = f32[768,128]{1,0:T(8,128)} custom-call(f32[512,128]{1,0:T(8,128)} %basis_ref.3, bf16[4,256,128]{2,1,0:T(8,128)(2,1)} %bitcast.11), custom_call_target="tpu_custom_call" | custom-call | tf_op jit(solution)/shard_map/pallas_call | solution.py:242
  38.8 1.0 reshape.32
  39.8 0.1 copy.23
  39.9 5.5 %all_to_all.32 = f32[2,32,12,128]{3,1,2,0:T(8,128)S(1)} all-to-all(f32[2,32,12,128]{3,1,2,0:T(8,128)S(1)} %copy.23), channel_id=1, replica_groups=mesh['item_0'=8,'item_1'=4,'item_2'=2,'user'=4] {'item_2'}, dimensions={0} | all-to-all | bytes 786432 | tf_op jit(solution)/shard_map/all_to_all | solution.py:265
  45.5 0.1 copy.24
  45.6 14.8 %all_to_all.33 = f32[32,12,128]{2,1,0:T(8,128)S(1)} all-to-all(f32[32,12,128]{2,1,0:T(8,128)S(1)} %copy.24), channel_id=1, replica_groups=mesh['item_0'=8,'item_1'=4,'item_2'=2,'user'=4] {'item_0','item_1'}, dimensions={0} | all-to-all | bytes 393216 | tf_op jit(solution)/shard_map/all_to_all | solution.py:266
  60.5 0.7 broadcast_in_dim.10
  61.2 0.0 copy-start.2
  61.2 4.4 %all-to-all-start.4 = ((f32[32,12,128]{2,1,0:T(8,128)}), f32[32,12,128]{2,1,0:T(8,128)S(1)}, u32[]{:S(2)}, u32[]{:S(2)}) async-start(f32[32,12,128]{2,1,0:T(8,128)} %broadcast_in_dim.10), calls=%async_computation.4 | async-start | bytes 524288 | tf_op jit(solution)/shard_map/all_to_all | solution.py:259
  65.6 0.0 copy-done.2
  65.6 0.1 copy.27.turn_ref
  65.7 10.2 %all-to-all-done.4 = f32[32,12,128]{2,1,0:T(8,128)S(1)} async-done(((f32[32,12,128]{2,1,0:T(8,128)}), f32[32,12,128]{2,1,0:T(8,128)S(1)}, u32[]{:S(2)}, u32[]{:S(2)}) %all-to-all-start.4) | async-done | bytes 196640 | tf_op jit(solution)/shard_map/all_to_all | solution.py:259
  76.0 0.1 copy.25
  76.1 7.2 %all_to_all.34 = f32[2,32,12,128]{3,1,2,0:T(8,128)S(1)} all-to-all(f32[2,32,12,128]{3,1,2,0:T(8,128)S(1)} %broadcast_in_dim.11), channel_id=1, replica_groups=mesh['item_0'=8,'item_1'=4,'item_2'=2,'user'=4] {'item_2'}, dimensions={0} | all-to-all | bytes 786432 | tf_op jit(solution)/shard_map/all_to_all | solution.py:259
  83.3 0.2 copy.26
  83.6 0.0 copy-start.1
  83.6 0.6 copy-done.1
  84.3 18.1 %shard_map.70 = (f32[128,384]{1,0:T(8,128)S(1)}, f32[256,128]{1,0:T(8,128)}) custom-call(f32[768,128]{1,0:T(8,128)S(1)} %reshape.33.sums_ref, f32[1,128]{1,0:T(1,128)S(1)} %bitcast.10, s32[256,1]{1,0:T(8,128)S(1)} %copy.27.turn_ref), custom_call_target="tpu_custom_call" | custom-call | tf_op jit(solution)/shard_map/pallas_call | solution.py:197
  102.4 0.0 copy-start
  102.4 0.7 copy-done
  103.1 2.9 %shard_map.71 = f32[512,128]{1,0:T(8,128)} custom-call(f32[512,128]{1,0:T(8,128)} %basis_ref.3, bf16[4,256,128]{2,1,0:T(8,128)(2,1)} %bitcast.12, f32[128,384]{1,0:T(8,128)} %copy-done), custom_call_target="tpu_custom_call" | custom-call | tf_op jit(solution)/shard_map/pallas_call | solution.py:254
  (7 shorter events, 0.2 us)
Async XLA Ops:
  61.2 4.4 %copy-start.2 = (s32[256]{0:T(256)S(1)}, s32[256]{0:T(256)}, u32[]{:S(2)}) copy-start(s32[256]{0:T(256)} %param.9) | copy-start | bytes 3076
  61.2 14.8 %all-to-all-start.4 = ((f32[32,12,128]{2,1,0:T(8,128)}), f32[32,12,128]{2,1,0:T(8,128)S(1)}, u32[]{:S(2)}, u32[]{:S(2)}) async-start(f32[32,12,128]{2,1,0:T(8,128)} %broadcast_in_dim.10), calls=%async_computation.4 | async-start | bytes 524288 | tf_op jit(solution)/shard_map/all_to_all | solution.py:259
  83.6 0.7 copy-start.1
  102.4 0.7 copy-start
where the time goes:
time: 106 us
  blocking collectives  60.4 us (57%)
  Pallas kernels  25.5 us (24%)
  waiting for transfers between devices  10.2 us (10%)
  local copies, waits for them, and re-layouts  4.61 us (4%)
  starting transfers between devices  4.38 us (4%)
    all_to_all x1, blocking collectives, per_device(): lax.all_to_all(column.reshape(n_item, slab_blocks, width), ITEM, 0, 0, ti...  23.1 us
    pallas_call x1, Pallas kernels, core(): pl.pallas_call(functools.partial(core_kernel, items), out_shape=[jax.Shap...  18.1 us
    all_to_all x2, blocking collectives, copies(): return lax.all_to_all(x, axis, split_axis=0, concat_axis=0, tiled=True)  17 us
    all_to_all x1, blocking collectives, summed(): own = lax.all_to_all(near, far, 0, 0, tiled=True).sum(axis=0)  14.8 us
    all_to_all x1, waiting for transfers between devices, copies(): return lax.all_to_all(x, axis, split_axis=0, concat_axis=0, tiled=True)  10.2 us
    all_to_all x1, blocking collectives, summed(): near = lax.all_to_all(pieces, 'item_2', 0, 0, tiled=True).sum(axis=0)  5.52 us
    all_to_all x1, starting transfers between devices, copies(): return lax.all_to_all(x, axis, split_axis=0, concat_axis=0, tiled=True)  4.38 us
    pallas_call x1, Pallas kernels, new_rows(): pl.pallas_call(rows_kernel, out_shape=jax.ShapeDtypeStruct(basis.shape, f...  2.87 us
  transfers between devices with their start and end apart: 1, of which 1 were waited for; matrix products, arithmetic and copies ran while one was open for 0% of the time, Pallas kernels for 0%

commit v1 on v0

--- a/solution.py
+++ b/solution.py
@@ -13,15 +13,35 @@
 
 f32 = jnp.float32
 exact_mode = lax.Precision.HIGHEST
-RANK, USERS, ORDER = 128, 256, 384
+RANK, USERS, ORDER, CAP = 128, 256, 384, 4
+
+
+def split(x):
+    high = x.astype(jnp.bfloat16)
+    rest = x - high.astype(f32)
+    middle = rest.astype(jnp.bfloat16)
+    return high, middle, (rest - middle.astype(f32)).astype(jnp.bfloat16)
+
+
+def product(a, b, dims):
+    n = a[0].shape[0]
+    one = lambda x, y: lax.dot_general(x, y, (dims, ((), ())), preferred_element_type=f32)
+    p = one(jnp.concatenate(a, axis=0), b[0])
+    q = one(jnp.concatenate(a[:2], axis=0), b[1])
+    r = one(a[0], b[2])
+    return p[:n] + ((p[n : 2 * n] + q[:n]) + ((p[2 * n :] + q[n:]) + r))
 
 
 def mm(a, b):
-    return jnp.dot(a, b, precision=exact_mode, preferred_element_type=f32)
+    a = a if isinstance(a, tuple) else split(a)
+    b = b if isinstance(b, tuple) else split(b)
+    return product(a, b, ((1,), (0,)))
 
 
 def mm_nt(a, b):
-    return lax.dot_general(a, b, (((1,), (1,)), ((), ())), precision=exact_mode, preferred_element_type=f32)
+    a = a if isinstance(a, tuple) else split(a)
+    b = b if isinstance(b, tuple) else split(b)
+    return product(a, b, ((1,), (1,)))
 
 
 def spread(x):
@@ -39,30 +59,39 @@
         first = 8 * panel
         column = [spread(here[:, first + k : first + k + 1]) for k in range(8)]
         pivot_of_row = jnp.ones((8, RANK), f32)
-        kept, inverses, uppers = [], [], []
-        for s in range(8):
+        steps = []
+        for s in range(0, 8, 2):
             upper = [spread(column[k][s : s + 1, :]) for k in range(s, 8)]
-            inverse = 1.0 / upper[0]
+            under = [spread(column[k][s + 1 : s + 2, :]) for k in range(s + 1, 8)]
+            a, b, c = upper[0], upper[1], under[0]
+            det = a * c - b * b
+            inverse = 1.0 / a
+            second = 1.0 / det
+            ratio = b * inverse
             line = spread(here[s : s + 1, :])
-            pivot_of_row = jnp.where(sub == s, upper[0], pivot_of_row)
             line = jnp.where(lane == first + s, line + line, line)
-            kept.append(line)
-            inverses.append(inverse)
-            uppers.append(upper)
-            factor = jnp.where(sub > s, column[s] * inverse, 0.0)
-            here = here - factor * line
-            for k in range(s + 1, 8):
-                column[k] = column[k] - factor * upper[k - s]
+            next_line = spread(here[s + 1 : s + 2, :]) - ratio * line
+            next_line = jnp.where(lane == first + s + 1, next_line + next_line, next_line)
+            pivot_of_row = jnp.where(sub == s, a, jnp.where(sub == s + 1, det * inverse, pivot_of_row))
+            next_inverse, mixed = a * second, b * second
+            under = [x - ratio * y for x, y in zip(under, upper[1:])]
+            steps.append((inverse, line, upper))
+            steps.append((next_inverse, next_line, under))
+            one = jnp.where(sub > s, column[s] * inverse, 0.0)
+            two = jnp.where(sub > s + 1, column[s + 1] * next_inverse - column[s] * mixed, 0.0)
+            here = here - one * line - two * next_line
+            for k in range(s + 2, 8):
+                column[k] = column[k] - one * upper[k - s] - two * under[k - s - 1]
         rows[panel] = here
         pivots.append(pivot_of_row)
         for other in range(panel + 1, count):
             there = rows[other]
             column = [spread(there[:, first + k : first + k + 1]) for k in range(8)]
-            for s in range(8):
-                factor = column[s] * inverses[s]
-                there = there - factor * kept[s]
+            for s, (inverse, line, upper) in enumerate(steps):
+                factor = column[s] * inverse
+                there = there - factor * line
                 for k in range(s + 1, 8):
-                    column[k] = column[k] - factor * uppers[s][k - s]
+                    column[k] = column[k] - factor * upper[k - s]
             rows[other] = there
     return lower_of(jnp.concatenate(rows, axis=0)), jnp.concatenate(pivots, axis=0)
 
@@ -136,14 +165,25 @@
     return whole * (1.0 / size), size
 
 
-def core_kernel(items, sums_ref, weights_ref, turn_ref, left_ref, factors_ref, gram_ref, turn_t_ref, back_ref):
+def core_kernel(
+    items, at_ref, near_ref, far1_ref, far2_ref, far3_ref, wide_ref, weights_ref, place_ref,
+    rows_ref, factors_ref, sums_ref, gram_ref, turn_t_ref, back_ref,
+):
+    half, ring = at_ref[0], at_ref[1]
+    piece = near_ref.shape[1]
+    for k, ref in enumerate((near_ref, far1_ref, far2_ref, far3_ref)):
+        chunk = lax.rem(ring + 4 - k, 4)
+        for j in range(2):
+            first = ((half if j == 0 else 1 - half) * 4 + chunk) * piece
+            sums_ref[pl.ds(pl.multiple_of(first, 8), piece), :] = ref[j]
     weights = weights_ref[...]
     whole, size = assemble(sums_ref, weights, items)
     gram_ref[...] = whole
-    g = gram_ref[...]
-
-    x = g[:RANK, :]
-    h1 = mm_nt(x, x)
+    g = split(whole)
+
+    x = whole[:RANK, :]
+    first = tuple(part[:RANK, :] for part in g)
+    h1 = mm_nt(first, first)
     low1, piv1 = eliminate(h1)
     x = turned(low1, piv1, x)
     x = mm(x, g)
@@ -186,20 +226,28 @@
 
     scale = lax.rsqrt(size)
     x = turn_t_ref[...] * scale
-    left_ref[:, :RANK] = x[:, :RANK] * weights
-    left_ref[:, RANK:] = x[:, RANK:]
-    user_of = turn_ref[...]
+    left = jnp.concatenate([x[:, :RANK] * weights, x[:, RANK:]], axis=1)
+    rows_ref[...] = mm_nt(wide_ref[...], left)
+    user_of = place_ref[...]
     onehot = jnp.where(lax.broadcasted_iota(jnp.int32, (USERS, USERS), 1) == user_of, 1.0, 0.0)
     factors_ref[...] = mm_nt(onehot, back_ref[:, RANK:] * (scale * size))
 
 
-def core(sums, weights, user_row, items):
+def core(at, pieces, wide, weights, place, items):
+    in_vmem = pl.BlockSpec(memory_space=pltpu.VMEM)
+    count, order = wide.shape
     return pl.pallas_call(
         functools.partial(core_kernel, items),
-        out_shape=[jax.ShapeDtypeStruct((RANK, ORDER), f32), jax.ShapeDtypeStruct((USERS, RANK), f32)],
-        scratch_shapes=[pltpu.VMEM((ORDER, ORDER), f32), pltpu.VMEM((RANK, ORDER), f32), pltpu.VMEM((RANK, ORDER), f32)],
+        out_shape=[jax.ShapeDtypeStruct((count, RANK), f32), jax.ShapeDtypeStruct((USERS, RANK), f32)],
+        in_specs=[pl.BlockSpec(memory_space=pltpu.SMEM)] + [in_vmem] * 7,
+        scratch_shapes=[
+            pltpu.VMEM((2 * order, RANK), f32),
+            pltpu.VMEM((order, order), f32),
+            pltpu.VMEM((RANK, order), f32),
+            pltpu.VMEM((RANK, order), f32),
+        ],
         compiler_params=pltpu.CompilerParams(vmem_limit_bytes=32 * 2**20),
-    )(sums, weights.reshape(1, RANK), user_row.reshape(USERS, 1))
+    )(at, *pieces, wide, weights.reshape(1, RANK), place.reshape(-1, 1))
 
 
 def column_kernel(row_ref, user_row_ref, blocks_ref, tiles_ref, out_ref):
@@ -222,50 +270,83 @@
     )(row.reshape(1), user_row.reshape(1, -1), block_ids.T, tiles)
 
 
-def gram_kernel(basis_ref, slab_ref, out_ref):
-    width = slab_ref.shape[2]
-    own = left = cross = 0.0
-    for b in range(slab_ref.shape[0]):
-        rows = basis_ref[width * b : width * (b + 1), :]
-        x = slab_ref[b]
-        own = own + lax.dot_general(rows, rows, (((0,), (0,)), ((), ())), precision=exact_mode, preferred_element_type=f32)
-        left = left + mm(x.astype(f32), rows)
-        cross = cross + lax.dot_general(x, x, (((1,), (1,)), ((), ())), preferred_element_type=f32)
-    out_ref[0:128, :] = own
-    out_ref[128:384, :] = left
-    out_ref[384:512, :] = cross[:128, :128]
-    out_ref[512:640, :] = cross[:128, 128:]
-    out_ref[640:768, :] = cross[128:, 128:]
-
-
-def gram_parts(basis, slab):
-    return pl.pallas_call(gram_kernel, out_shape=jax.ShapeDtypeStruct((768, RANK), f32))(basis, slab)
-
-
-def rows_kernel(basis_ref, slab_ref, left_ref, out_ref):
-    width = slab_ref.shape[2]
-    for b in range(slab_ref.shape[0]):
-        here = slice(width * b, width * (b + 1))
-        x = jnp.transpose(slab_ref[b].astype(f32))
-        out_ref[here, :] = mm_nt(basis_ref[here, :], left_ref[:, :RANK]) + mm_nt(x, left_ref[:, RANK:])
-
-
-def new_rows(basis, slab, left):
-    return pl.pallas_call(rows_kernel, out_shape=jax.ShapeDtypeStruct(basis.shape, f32))(basis, slab, left)
-
-
-def copies(x, axis):
-    x = jnp.broadcast_to(x, (lax.axis_size(axis), *x.shape))
-    return lax.all_to_all(x, axis, split_axis=0, concat_axis=0, tiled=True)
-
-
-def summed(parts):
-    far = ("item_0", "item_1")
-    pieces = parts.reshape(2, lax.axis_size(far), -1, RANK)
-    near = lax.all_to_all(pieces, "item_2", 0, 0, tiled=True).sum(axis=0)
-    own = lax.all_to_all(near, far, 0, 0, tiled=True).sum(axis=0)
-    half = copies(own, far)
-    return copies(half, "item_2").reshape(parts.shape)
+def strips(refs, flat_ref):
+    pieces = []
+    for ref in refs:
+        flat_ref[...] = ref[...].astype(f32)
+        count = flat_ref.shape[0] // CAP
+        blocks = [flat_ref[pl.ds(b, count, stride=CAP), :] for b in range(CAP)]
+        pieces.append(jnp.concatenate(blocks, axis=1))
+    return jnp.concatenate(pieces, axis=0)
+
+
+def gram_kernel(at_ref, basis_ref, x0_ref, x1_ref, x2_ref, x3_ref, keep_ref, send_ref, flat_ref):
+    x = strips((x0_ref, x1_ref, x2_ref, x3_ref), flat_ref).astype(jnp.bfloat16)
+    parts = split(basis_ref[...])
+    high_t, middle_t = (jnp.transpose(p.astype(f32)).astype(jnp.bfloat16) for p in parts[:2])
+    one = lambda a, b: jnp.dot(a, b, preferred_element_type=f32)
+    both = one(jnp.concatenate([x, high_t], axis=0), jnp.concatenate(parts, axis=1))
+    strip = lambda rows, k: both[rows, RANK * k : RANK * (k + 1)]
+    users, rest = slice(0, USERS), slice(USERS, None)
+    left = strip(users, 0) + (strip(users, 1) + strip(users, 2))
+    small = strip(rest, 1) + strip(rest, 2)
+    own = strip(rest, 0) + (small + jnp.transpose(small) + one(middle_t, parts[1]))
+    cross = lax.dot_general(x, x, (((1,), (1,)), ((), ())), preferred_element_type=f32)
+    low = [own, left[:RANK], left[RANK:]]
+    high = [cross[:RANK, :RANK], cross[:RANK, RANK:], cross[RANK:, RANK:]]
+    half = at_ref[0]
+    for k in range(3):
+        keep_ref[RANK * k : RANK * (k + 1), :] = jnp.where(half == 0, low[k], high[k])
+        send_ref[RANK * k : RANK * (k + 1), :] = jnp.where(half == 0, high[k], low[k])
+
+
+def gram_parts(at, basis, pieces):
+    in_vmem = pl.BlockSpec(memory_space=pltpu.VMEM)
+    return pl.pallas_call(
+        gram_kernel,
+        out_shape=[jax.ShapeDtypeStruct((3 * RANK, RANK), f32)] * 2,
+        in_specs=[pl.BlockSpec(memory_space=pltpu.SMEM)] + [in_vmem] * 5,
+        scratch_shapes=[pltpu.VMEM(pieces[0].shape, f32)],
+        compiler_params=pltpu.CompilerParams(vmem_limit_bytes=32 * 2**20),
+    )(at, basis, *pieces)
+
+
+def wide_kernel(basis_ref, x0_ref, x1_ref, x2_ref, x3_ref, out_ref, flat_ref):
+    out_ref[:, :RANK] = basis_ref[...]
+    out_ref[:, RANK:] = jnp.transpose(strips((x0_ref, x1_ref, x2_ref, x3_ref), flat_ref))
+
+
+def wide_of(basis, pieces):
+    in_vmem = pl.BlockSpec(memory_space=pltpu.VMEM)
+    return pl.pallas_call(
+        wide_kernel,
+        out_shape=jax.ShapeDtypeStruct((basis.shape[0], RANK + USERS), f32),
+        in_specs=[in_vmem] * 5,
+        scratch_shapes=[pltpu.VMEM(pieces[0].shape, f32)],
+        compiler_params=pltpu.CompilerParams(vmem_limit_bytes=32 * 2**20),
+    )(basis, *pieces)
+
+
+def around(x, axis):
+    n = lax.axis_size(axis)
+    return [lax.ppermute(x, axis, [(i, (i + k) % n) for i in range(n)]) for k in range(1, n)]
+
+
+def summed(keep, send):
+    other = [(0, 1), (1, 0)]
+    total = keep + lax.ppermute(send, "item_2", other)
+    n = lax.axis_size("item_1")
+    rows = total.shape[0] // n
+    here = lax.axis_index("item_1")
+    part = lambda k: lax.dynamic_slice_in_dim(total, (here + k) % n * rows, rows)
+    own = part(0)
+    for k in range(1, n):
+        own = own + lax.ppermute(part(k), "item_1", [(i, (i + k) % n) for i in range(n)])
+    far = lax.axis_size("item_0")
+    every = lax.all_to_all(jnp.broadcast_to(own, (far, *own.shape)), "item_0", 0, 0, tiled=True)
+    own = jnp.sum(every, axis=0)
+    pair = jnp.stack([own, lax.ppermute(own, "item_2", other)])
+    return [pair] + around(pair, "item_1")
 
 
 def per_device(basis, old_values, ratings, block_ids, user_row):
@@ -276,12 +357,15 @@
     row = lax.axis_index(ITEM) * n_user + lax.axis_index("user")
     column = column_of(row, user_row, block_ids, ratings[0], n_item * slab_blocks)
     arrived = lax.all_to_all(column.reshape(n_item, slab_blocks, width), ITEM, 0, 0, tiled=True)
-    pooled = copies(arrived, "user")
-    slab = pooled.reshape(USERS, slab_blocks, width).swapaxes(0, 1)
-    sums = summed(gram_parts(basis, slab))
-    place = user_row % n_user * n_item + user_row // n_user
-    left, user_factors = core(sums, old_values, place, basis.shape[0] * n_item)
-    return new_rows(basis, slab, left), user_factors
+    arrived = arrived.reshape(n_item * slab_blocks, width)
+    pieces = [arrived] + around(arrived, "user")
+    at = jnp.stack([lax.axis_index("item_2"), lax.axis_index("item_1")]).astype(jnp.int32)
+    keep, send = gram_parts(at, basis, pieces)
+    wide = wide_of(basis, pieces)
+    sums = summed(keep, send)
+    steps = (lax.axis_index("user") - user_row % n_user) % n_user
+    place = steps * n_item + user_row // n_user
+    return tuple(core(at, sums, wide, old_values, place, basis.shape[0] * n_item))
 
 
 def solution(mesh):

time: 106 us -> 94.2 us (0.89)
  blocking collectives: 60.4 us -> 37.1 us
  starting transfers between devices: 4.38 us -> 13.4 us
  waiting for transfers between devices: 10.2 us -> 18.3 us
  local copies, waits for them, and re-layouts: 4.61 us -> 0.2 us
  Pallas kernels: 25.5 us -> 24.1 us
    all_to_all x4 -> x1, blocking collectives: 37.3 us -> 14.1 us  [summed(): lax.all_to_all(jnp.broadcast_to(own, (far, *own.shape)), 'item_0', 0, 0,...]
    ppermute x0 -> x11, waiting for transfers between devices: none -> 18.3 us  [the longest x6 11.9 us: around(): lax.ppermute(x, axis, [(i, (i + k) % n) for i in range(n)])]
    ppermute x0 -> x11, starting transfers between devices: none -> 13.4 us  [the longest x6 5.32 us: around(): lax.ppermute(x, axis, [(i, (i + k) % n) for i in range(n)])]
    all_to_all x1 -> x0, waiting for transfers between devices: 10.2 us -> none  [copies(): return lax.all_to_all(x, axis, split_axis=0, concat_axis=0, tiled=True)]
    all_to_all x1 -> x0, starting transfers between devices: 4.38 us -> none  [copies(): return lax.all_to_all(x, axis, split_axis=0, concat_axis=0, tiled=True)]
    pallas_call x2, Pallas kernels: 5.6 us -> 1.24 us  [the longest x1 1.09 us: gram_parts(): pl.pallas_call(gram_kernel, out_shape=[jax.ShapeDtypeStruct((3 * RANK, RA...]
    pallas_call x1, Pallas kernels: 18.1 us -> 21.1 us  [core(): pl.pallas_call(functools.partial(core_kernel, items), out_shape=[jax.Shap...]
    unnamed x6, local copies, waits for them, and re-layouts: 1.33 us -> 0.01 us
  transfers between devices with their start and end apart: 1 -> 11, of which waited for: 1 -> 10; matrix products, arithmetic and copies ran while one was open for 0% -> 0% of each run, Pallas kernels for 0% -> 0%
where the time goes in v1:
time: 94.2 us; the launch traced here: 94 us
  blocking collectives  37.1 us (39%)
  Pallas kernels  24.1 us (26%)
  waiting for transfers between devices  18.3 us (19%)
  starting transfers between devices  13.4 us (14%)
    all_to_all x1, blocking collectives, per_device(): lax.all_to_all(column.reshape(n_item, slab_blocks, width), ITEM, 0, 0, ti...  23.1 us
    pallas_call x1, Pallas kernels, core(): pl.pallas_call(functools.partial(core_kernel, items), out_shape=[jax.Shap...  21.1 us
    all_to_all x1, blocking collectives, summed(): lax.all_to_all(jnp.broadcast_to(own, (far, *own.shape)), 'item_0', 0, 0,...  14.1 us
    ppermute x6, waiting for transfers between devices, around(): lax.ppermute(x, axis, [(i, (i + k) % n) for i in range(n)])  11.9 us
    ppermute x6, starting transfers between devices, around(): lax.ppermute(x, axis, [(i, (i + k) % n) for i in range(n)])  5.32 us
    ppermute x3, waiting for transfers between devices, summed(): lax.ppermute(part(k), 'item_1', [(i, (i + k) % n) for i in range(n)])  4.44 us
    ppermute x1, starting transfers between devices, summed(): pair = jnp.stack([own, lax.ppermute(own, 'item_2', other)])  4.05 us
    ppermute x3, starting transfers between devices, summed(): lax.ppermute(part(k), 'item_1', [(i, (i + k) % n) for i in range(n)])  2.76 us
  transfers between devices with their start and end apart: 11, of which 10 were waited for; matrix products, arithmetic and copies ran while one was open for 0% of the time, Pallas kernels for 0%

profile of v1, /device:TPU:1, one launch (start us, length us, event | category | flops | bytes accessed | tf_op | source)
XLA Modules:
  0.0 94.0 jit_solution(8122875481450629515)
XLA Ops:
  0.6 0.0 copy-start
  0.7 1.8 %shard_map.68 = bf16[256,128]{1,0:T(8,128)(2,1)} custom-call(s32[1]{0:T(128)} %bitcast.2.row_ref, s32[1,256]{1,0:T(1,128)} %bitcast.23, s32[64,256]{1,0:T(8,128)} %bitcast.20, bf16[64,128]{1,0:T(8,128)(2,1)} %bitcast.22), custom_call_target="tpu_custom_call" | custom-call | tf_op jit(solution)/shard_map/pallas_call | solution.py:265
  2.5 23.1 %all_to_all.10 = bf16[64,4,128]{2,1,0:T(4,128)(2,1)S(1)} all-to-all(bf16[64,4,128]{2,1,0:T(4,128)(2,1)} %bitcast.18), channel_id=1, replica_groups=mesh['item_0'=8,'item_1'=4,'item_2'=2,'user'=4] {'item_0','item_1','item..., dimensions={0} | all-to-all | bytes 131072 | tf_op jit(solution)/shard_map/all_to_all | solution.py:359
  25.5 2.7 %collective-permute-start.2 = (bf16[256,128]{1,0:T(8,128)(2,1)S(1)}, bf16[256,128]{1,0:T(8,128)(2,1)S(1)}, u32[]{:S(2)}, u32[]{:S(2)}) collective-permute-start(bf16[256,128]{1,0:T(8,128)(2,1)S(1)} %bitcast.12), channel_id=1, source_target_pairs={{0,3},{1,0},{2,1},{3,2},{4,7},{5,4},{6,5},{7,6},{8,11},{9,8},{10,9... | collective-permute-start | bytes 196616 | tf_op jit(solution)/shard_map/ppermute | solution.py:332
  28.3 0.3 collective-permute-start.1
  28.6 0.7 collective-permute-start
  29.3 0.1 pad_add_fusion.at_ref
  29.4 0.2 collective-permute-done.2.x3_ref
  29.6 3.4 %collective-permute-done.1.x2_ref = bf16[256,128]{1,0:T(8,128)(2,1)S(1)} collective-permute-done((bf16[256,128]{1,0:T(8,128)(2,1)S(1)}, bf16[256,128]{1,0:T(8,128)(2,1)S(1)}, u32[]{:S(2)}, u32[]{:S(2)}) %collective-permute-start.1) | collective-permute-done | bytes 65568 | tf_op jit(solution)/shard_map/ppermute | solution.py:332
  32.9 1.6 %collective-permute-done.x1_ref = bf16[256,128]{1,0:T(8,128)(2,1)S(1)} collective-permute-done((bf16[256,128]{1,0:T(8,128)(2,1)S(1)}, bf16[256,128]{1,0:T(8,128)(2,1)S(1)}, u32[]{:S(2)}, u32[]{:S(2)}) %collective-permute-start) | collective-permute-done | bytes 65568 | tf_op jit(solution)/shard_map/ppermute | solution.py:332
  34.5 1.1 %shard_map.69 = (f32[384,128]{1,0:T(8,128)S(1)}, f32[384,128]{1,0:T(8,128)S(1)}) custom-call(s32[2]{0:T(128)S(1)} %pad_add_fusion.at_ref, f32[512,128]{1,0:T(8,128)S(1)} %copy-done, bf16[256,128]{1,0:T(8,128)(2,1)S(1)} %bitcast.15, bf16[256,128]{1,0:T(8,128)(2,1)S(1)} %collective-permute-done.x1_ref, bf16[256,128]{1,0:T(8,128)(2,1)S(1)} %collective-permute-done.1.x2_ref, ...), custom_call_target="tpu_custom_call" | custom-call | tf_op jit(solution)/shard_map/pallas_call | solution.py:305
  35.6 1.3 %collective-permute-start.3 = (f32[384,128]{1,0:T(8,128)S(1)}, f32[384,128]{1,0:T(8,128)S(1)}, u32[]{:S(2)}, u32[]{:S(2)}) collective-permute-start(f32[384,128]{1,0:T(8,128)S(1)} %get-tuple-element.5), channel_id=1, source_target_pairs={{0,4},{4,0},{1,5},{5,1},{2,6},{6,2},{3,7},{7,3},{8,12},{12,8},{9,1... | collective-permute-start | bytes 589832 | tf_op jit(solution)/shard_map/ppermute | solution.py:337
  36.9 1.1 %collective-permute-done.3 = f32[384,128]{1,0:T(8,128)S(1)} collective-permute-done((f32[384,128]{1,0:T(8,128)S(1)}, f32[384,128]{1,0:T(8,128)S(1)}, u32[]{:S(2)}, u32[]{:S(2)}) %collective-permute-start.3) | collective-permute-done | bytes 196640 | tf_op jit(solution)/shard_map/ppermute | solution.py:337
  38.0 0.3 collective-permute-start.4
  38.3 2.5 %collective-permute-start.6 = (f32[96,128]{1,0:T(8,128)S(1)}, f32[96,128]{1,0:T(8,128)S(1)}, u32[]{:S(2)}, u32[]{:S(2)}) collective-permute-start(f32[96,128]{1,0:T(8,128)S(1)} %get-tuple-element.7), channel_id=1, source_target_pairs={{0,24},{8,0},{16,8},{24,16},{1,25},{9,1},{17,9},{25,17},{2,26},{10... | collective-permute-start | bytes 147464 | tf_op jit(solution)/shard_map/ppermute | solution.py:344
  40.7 0.0 collective-permute-start.5
  40.8 1.5 %collective-permute-done.4 = f32[96,128]{1,0:T(8,128)S(1)} collective-permute-done((f32[96,128]{1,0:T(8,128)S(1)}, f32[96,128]{1,0:T(8,128)S(1)}, u32[]{:S(2)}, u32[]{:S(2)}) %collective-permute-start.4) | collective-permute-done | bytes 49184 | tf_op jit(solution)/shard_map/ppermute | solution.py:344
  42.2 0.0 collective-permute-done.6
  42.2 3.0 %collective-permute-done.5 = f32[96,128]{1,0:T(8,128)S(1)} collective-permute-done((f32[96,128]{1,0:T(8,128)S(1)}, f32[96,128]{1,0:T(8,128)S(1)}, u32[]{:S(2)}, u32[]{:S(2)}) %collective-permute-start.5) | collective-permute-done | bytes 49184 | tf_op jit(solution)/shard_map/ppermute | solution.py:344
  45.2 14.1 %all_to_all.11 = f32[8,96,128]{2,1,0:T(8,128)S(1)} all-to-all(f32[8,96,128]{2,1,0:T(8,128)S(1)} %broadcast_in_dim.3), channel_id=1, replica_groups=mesh['item_0'=8,'item_1'=4,'item_2'=2,'user'=4] {'item_0'}, dimensions={0} | all-to-all | bytes 786432 | tf_op jit(solution)/shard_map/all_to_all | solution.py:346
  59.3 4.0 %collective-permute-start.7 = (f32[96,128]{1,0:T(8,128)S(1)}, f32[96,128]{1,0:T(8,128)S(1)}, u32[]{:S(2)}, u32[]{:S(2)}) collective-permute-start(f32[96,128]{1,0:T(8,128)S(1)} %reduce_sum.9), channel_id=1, source_target_pairs={{0,4},{4,0},{1,5},{5,1},{2,6},{6,2},{3,7},{7,3},{8,12},{12,8},{9,1... | collective-permute-start | bytes 147464 | tf_op jit(solution)/shard_map/ppermute | solution.py:348
  63.4 0.9 collective-permute-done.7
  64.3 0.3 collective-permute-start.10
  64.6 0.5 collective-permute-start.9
  65.1 0.7 collective-permute-start.8
  65.8 0.1 copy.8.place_ref
  66.0 0.2 shard_map.70.wide_ref
  66.2 0.0 copy-start.1
  66.2 2.2 %collective-permute-done.10.far3_ref = f32[2,96,128]{2,1,0:T(8,128)S(1)} collective-permute-done((f32[2,96,128]{2,1,0:T(8,128)S(1)}, f32[2,96,128]{2,1,0:T(8,128)S(1)}, u32[]{:S(2)}, u32[]{:S(2)}) %collective-permute-start.10) | collective-permute-done | bytes 98336 | tf_op jit(solution)/shard_map/ppermute | solution.py:332
  68.4 1.2 %collective-permute-done.9.far2_ref = f32[2,96,128]{2,1,0:T(8,128)S(1)} collective-permute-done((f32[2,96,128]{2,1,0:T(8,128)S(1)}, f32[2,96,128]{2,1,0:T(8,128)S(1)}, u32[]{:S(2)}, u32[]{:S(2)}) %collective-permute-start.9) | collective-permute-done | bytes 98336 | tf_op jit(solution)/shard_map/ppermute | solution.py:332
  69.6 3.3 %collective-permute-done.8.far1_ref = f32[2,96,128]{2,1,0:T(8,128)S(1)} collective-permute-done((f32[2,96,128]{2,1,0:T(8,128)S(1)}, f32[2,96,128]{2,1,0:T(8,128)S(1)}, u32[]{:S(2)}, u32[]{:S(2)}) %collective-permute-start.8) | collective-permute-done | bytes 98336 | tf_op jit(solution)/shard_map/ppermute | solution.py:332
  72.9 21.1 %shard_map.71 = (f32[512,128]{1,0:T(8,128)}, f32[256,128]{1,0:T(8,128)}) custom-call(s32[2]{0:T(128)S(1)} %pad_add_fusion.at_ref, f32[2,96,128]{2,1,0:T(8,128)S(1)} %pad_maximum_fusion.near_ref, f32[2,96,128]{2,1,0:T(8,128)S(1)} %collective-permute-done.8.far1_ref, f32[2,96,128]{2,1,0:T(8,128)S(1)} %collective-permute-done.9.far2_ref, ...), custom_call_target="tpu_custom_call" | custom-call | tf_op jit(solution)/shard_map/pallas_call | solution.py:239
  (11 shorter events, 0.2 us)
Async XLA Ops:
  0.6 33.9 %copy-start = (f32[512,128]{1,0:T(8,128)S(1)}, f32[512,128]{1,0:T(8,128)}, u32[]{:S(2)}) copy-start(f32[512,128]{1,0:T(8,128)} %basis_ref.3) | copy-start | bytes 786436
  25.5 4.1 %collective-permute-start.2 = (bf16[256,128]{1,0:T(8,128)(2,1)S(1)}, bf16[256,128]{1,0:T(8,128)(2,1)S(1)}, u32[]{:S(2)}, u32[]{:S(2)}) collective-permute-start(bf16[256,128]{1,0:T(8,128)(2,1)S(1)} %bitcast.12), channel_id=1, source_target_pairs={{0,3},{1,0},{2,1},{3,2},{4,7},{5,4},{6,5},{7,6},{8,11},{9,8},{10,9... | collective-permute-start | bytes 196616 | tf_op jit(solution)/shard_map/ppermute | solution.py:332
  28.3 4.7 %collective-permute-start.1 = (bf16[256,128]{1,0:T(8,128)(2,1)S(1)}, bf16[256,128]{1,0:T(8,128)(2,1)S(1)}, u32[]{:S(2)}, u32[]{:S(2)}) collective-permute-start(bf16[256,128]{1,0:T(8,128)(2,1)S(1)} %bitcast.13), channel_id=1, source_target_pairs={{0,2},{1,3},{2,0},{3,1},{4,6},{5,7},{6,4},{7,5},{8,10},{9,11},{10,... | collective-permute-start | bytes 196616 | tf_op jit(solution)/shard_map/ppermute | solution.py:332
  28.6 5.9 %collective-permute-start = (bf16[256,128]{1,0:T(8,128)(2,1)S(1)}, bf16[256,128]{1,0:T(8,128)(2,1)S(1)}, u32[]{:S(2)}, u32[]{:S(2)}) collective-permute-start(bf16[256,128]{1,0:T(8,128)(2,1)S(1)} %bitcast.14), channel_id=1, source_target_pairs={{0,1},{1,2},{2,3},{3,0},{4,5},{5,6},{6,7},{7,4},{8,9},{9,10},{10,1... | collective-permute-start | bytes 196616 | tf_op jit(solution)/shard_map/ppermute | solution.py:332
  35.6 2.3 %collective-permute-start.3 = (f32[384,128]{1,0:T(8,128)S(1)}, f32[384,128]{1,0:T(8,128)S(1)}, u32[]{:S(2)}, u32[]{:S(2)}) collective-permute-start(f32[384,128]{1,0:T(8,128)S(1)} %get-tuple-element.5), channel_id=1, source_target_pairs={{0,4},{4,0},{1,5},{5,1},{2,6},{6,2},{3,7},{7,3},{8,12},{12,8},{9,1... | collective-permute-start | bytes 589832 | tf_op jit(solution)/shard_map/ppermute | solution.py:337
  38.0 4.2 %collective-permute-start.4 = (f32[96,128]{1,0:T(8,128)S(1)}, f32[96,128]{1,0:T(8,128)S(1)}, u32[]{:S(2)}, u32[]{:S(2)}) collective-permute-start(f32[96,128]{1,0:T(8,128)S(1)} %get-tuple-element.6), channel_id=1, source_target_pairs={{0,8},{8,16},{16,24},{24,0},{1,9},{9,17},{17,25},{25,1},{2,10},{10... | collective-permute-start | bytes 147464 | tf_op jit(solution)/shard_map/ppermute | solution.py:344
  38.3 4.0 %collective-permute-start.6 = (f32[96,128]{1,0:T(8,128)S(1)}, f32[96,128]{1,0:T(8,128)S(1)}, u32[]{:S(2)}, u32[]{:S(2)}) collective-permute-start(f32[96,128]{1,0:T(8,128)S(1)} %get-tuple-element.7), channel_id=1, source_target_pairs={{0,24},{8,0},{16,8},{24,16},{1,25},{9,1},{17,9},{25,17},{2,26},{10... | collective-permute-start | bytes 147464 | tf_op jit(solution)/shard_map/ppermute | solution.py:344
  40.7 4.4 %collective-permute-start.5 = (f32[96,128]{1,0:T(8,128)S(1)}, f32[96,128]{1,0:T(8,128)S(1)}, u32[]{:S(2)}, u32[]{:S(2)}) collective-permute-start(f32[96,128]{1,0:T(8,128)S(1)} %get-tuple-element.8), channel_id=1, source_target_pairs={{0,16},{8,24},{16,0},{24,8},{1,17},{9,25},{17,1},{25,9},{2,18},{10... | collective-permute-start | bytes 147464 | tf_op jit(solution)/shard_map/ppermute | solution.py:344
  59.3 4.9 %collective-permute-start.7 = (f32[96,128]{1,0:T(8,128)S(1)}, f32[96,128]{1,0:T(8,128)S(1)}, u32[]{:S(2)}, u32[]{:S(2)}) collective-permute-start(f32[96,128]{1,0:T(8,128)S(1)} %reduce_sum.9), channel_id=1, source_target_pairs={{0,4},{4,0},{1,5},{5,1},{2,6},{6,2},{3,7},{7,3},{8,12},{12,8},{9,1... | collective-permute-start | bytes 147464 | tf_op jit(solution)/shard_map/ppermute | solution.py:348
  64.3 1.6 %copy-start.2 = (s32[256]{0:T(256)S(1)}, s32[256]{0:T(256)}, u32[]{:S(2)}) copy-start(s32[256]{0:T(256)} %param.9) | copy-start | bytes 3076
  64.3 4.1 %collective-permute-start.10 = (f32[2,96,128]{2,1,0:T(8,128)S(1)}, f32[2,96,128]{2,1,0:T(8,128)S(1)}, u32[]{:S(2)}, u32[]{:S(2)}) collective-permute-start(f32[2,96,128]{2,1,0:T(8,128)S(1)} %pad_maximum_fusion.near_ref), channel_id=1, source_target_pairs={{0,24},{8,0},{16,8},{24,16},{1,25},{9,1},{17,9},{25,17},{2,26},{10... | collective-permute-start | bytes 294920 | tf_op jit(solution)/shard_map/ppermute | solution.py:332
  64.6 5.0 %collective-permute-start.9 = (f32[2,96,128]{2,1,0:T(8,128)S(1)}, f32[2,96,128]{2,1,0:T(8,128)S(1)}, u32[]{:S(2)}, u32[]{:S(2)}) collective-permute-start(f32[2,96,128]{2,1,0:T(8,128)S(1)} %pad_maximum_fusion.near_ref), channel_id=1, source_target_pairs={{0,16},{8,24},{16,0},{24,8},{1,17},{9,25},{17,1},{25,9},{2,18},{10... | collective-permute-start | bytes 294920 | tf_op jit(solution)/shard_map/ppermute | solution.py:332
  65.1 7.8 %collective-permute-start.8 = (f32[2,96,128]{2,1,0:T(8,128)S(1)}, f32[2,96,128]{2,1,0:T(8,128)S(1)}, u32[]{:S(2)}, u32[]{:S(2)}) collective-permute-start(f32[2,96,128]{2,1,0:T(8,128)S(1)} %pad_maximum_fusion.near_ref), channel_id=1, source_target_pairs={{0,8},{8,16},{16,24},{24,0},{1,9},{9,17},{17,25},{25,1},{2,10},{10... | collective-permute-start | bytes 294920 | tf_op jit(solution)/shard_map/ppermute | solution.py:332
  66.2 6.8 %copy-start.1 = (f32[128]{0:T(128)S(1)}, f32[128]{0:T(128)}, u32[]{:S(2)}) copy-start(f32[128]{0:T(128)} %param.6) | copy-start | bytes 1540

commit v2 on v1

--- a/solution.py
+++ b/solution.py
@@ -12,7 +12,6 @@
 ITEM_USER = ("item_0", "item_1", "item_2", "user")
 
 f32 = jnp.float32
-exact_mode = lax.Precision.HIGHEST
 RANK, USERS, ORDER, CAP = 128, 256, 384, 4
 
 
@@ -107,23 +106,6 @@
     return jnp.where(i >= k, x, 0.0)
 
 
-def eliminate_slowly(gram):
-    i, k = square_iotas()
-
-    def step(j, carry):
-        x, pivots = carry
-        line = jnp.sum(jnp.where(i == j, x, 0.0), axis=0, keepdims=True)
-        column = jnp.sum(jnp.where(k == j, x, 0.0), axis=1, keepdims=True)
-        pivot = jnp.sum(jnp.where((i == j) & (k == j), x, 0.0), axis=(0, 1), keepdims=True)
-        pivots = jnp.where(i == j, pivot, pivots)
-        doubled = jnp.where(k[:1] == j, line + line, line)
-        x = x - jnp.where(i > j, column / pivot, 0.0) * doubled
-        return x, pivots
-
-    x, pivots = lax.fori_loop(0, RANK, step, (gram, jnp.ones((RANK, RANK), f32)))
-    return lower_of(x), pivots
-
-
 def scaled(x, pivots, power):
     factor = 1.0 / pivots if power == 1 else lax.rsqrt(pivots)
     return jnp.concatenate([x[:, c : c + RANK] * factor for c in range(0, x.shape[1], RANK)], axis=1)
@@ -166,16 +148,13 @@
 
 
 def core_kernel(
-    items, at_ref, near_ref, far1_ref, far2_ref, far3_ref, wide_ref, weights_ref, place_ref,
+    items, at_ref, near_ref, far_ref, wide_ref, weights_ref, place_ref,
     rows_ref, factors_ref, sums_ref, gram_ref, turn_t_ref, back_ref,
 ):
-    half, ring = at_ref[0], at_ref[1]
-    piece = near_ref.shape[1]
-    for k, ref in enumerate((near_ref, far1_ref, far2_ref, far3_ref)):
-        chunk = lax.rem(ring + 4 - k, 4)
-        for j in range(2):
-            first = ((half if j == 0 else 1 - half) * 4 + chunk) * piece
-            sums_ref[pl.ds(pl.multiple_of(first, 8), piece), :] = ref[j]
+    piece = near_ref.shape[0]
+    for k, ref in enumerate((near_ref, far_ref)):
+        first = piece * (at_ref[0] if k == 0 else 1 - at_ref[0])
+        sums_ref[pl.ds(pl.multiple_of(first, 8), piece), :] = ref[...]
     weights = weights_ref[...]
     whole, size = assemble(sums_ref, weights, items)
     gram_ref[...] = whole
@@ -197,57 +176,59 @@
     low3, piv3 = eliminate(h3)
     turn_t_ref[...] = turned(low3, piv3, x)
     back_ref[...] = turned(low3, piv3, y)
-    fine = (smallest(piv1, h1) > 1e-4) & (smallest(piv2, h2) > 3e-4) & (smallest(piv3, h3) > 8e-3)
+    last = smallest(piv3, h3)
+    fine = (smallest(piv1, h1) > 3e-5) & (smallest(piv2, h2) > 1e-5) & (last > 1e-4)
 
     @pl.when(jnp.logical_not(fine))
     def _():
-        def ortho(x, y):
-            gram = mm_nt(x, y)
-            return eliminate_slowly(gram)
-
-        def sweep(n, x):
-            y = mm(x, gram_ref[...])
-            low, piv = ortho(x, y)
-            y = turned(low, piv, y)
-            low, piv = ortho(y, y)
-            return turned(low, piv, y)
+        def turn(n, x):
+            even = lax.rem(n, 2) == 0
+            y = jnp.where(even, mm(x, split(gram_ref[...])), x)
+            low, piv = eliminate(mm_nt(x, y))
+            back = turned(low, piv, y)
+            turn_t_ref[...] = turned(low, piv, x)
+            back_ref[...] = back
+            return back
 
         start = jnp.where(
             lax.broadcasted_iota(jnp.int32, (RANK, ORDER), 0) == lax.broadcasted_iota(jnp.int32, (RANK, ORDER), 1), 1.0, 0.0
         )
-        x = lax.fori_loop(0, 4, sweep, start)
-        y = mm(x, gram_ref[...])
-        low, piv = ortho(x, y)
-        x, y = turned(low, piv, x), turned(low, piv, y)
-        x, y = polished(x, y)
-        x, y = polished(x, y)
+        lax.fori_loop(0, 9, turn, start)
+
+    @pl.when(jnp.logical_not(fine & (last > 2e-2)))
+    def _():
+        x, y = polished(turn_t_ref[...], back_ref[...])
         turn_t_ref[...] = x
         back_ref[...] = y
 
     scale = lax.rsqrt(size)
     x = turn_t_ref[...] * scale
-    left = jnp.concatenate([x[:, :RANK] * weights, x[:, RANK:]], axis=1)
-    rows_ref[...] = mm_nt(wide_ref[...], left)
+    left = split(jnp.concatenate([x[:, :RANK] * weights, x[:, RANK:]], axis=1))
+    one = lambda a, b: lax.dot_general(a, b, (((1,), (1,)), ((), ())), preferred_element_type=f32)
+    most = one(wide_ref[:, :ORDER], jnp.concatenate(left, axis=0))
+    some = one(wide_ref[:, ORDER : ORDER + RANK], jnp.concatenate([p[:, :RANK] for p in left[:2]], axis=0))
+    least = one(wide_ref[:, ORDER + RANK :], left[0][:, :RANK])
+    strip = lambda y, k: y[:, RANK * k : RANK * (k + 1)]
+    rows_ref[...] = strip(most, 0) + ((strip(most, 1) + strip(some, 0)) + (strip(most, 2) + strip(some, 1) + least))
     user_of = place_ref[...]
     onehot = jnp.where(lax.broadcasted_iota(jnp.int32, (USERS, USERS), 1) == user_of, 1.0, 0.0)
     factors_ref[...] = mm_nt(onehot, back_ref[:, RANK:] * (scale * size))
 
 
-def core(at, pieces, wide, weights, place, items):
+def core(at, near, far, wide, weights, place, items):
     in_vmem = pl.BlockSpec(memory_space=pltpu.VMEM)
-    count, order = wide.shape
     return pl.pallas_call(
         functools.partial(core_kernel, items),
-        out_shape=[jax.ShapeDtypeStruct((count, RANK), f32), jax.ShapeDtypeStruct((USERS, RANK), f32)],
-        in_specs=[pl.BlockSpec(memory_space=pltpu.SMEM)] + [in_vmem] * 7,
+        out_shape=[jax.ShapeDtypeStruct((wide.shape[0], RANK), f32), jax.ShapeDtypeStruct((USERS, RANK), f32)],
+        in_specs=[pl.BlockSpec(memory_space=pltpu.SMEM)] + [in_vmem] * 5,
         scratch_shapes=[
-            pltpu.VMEM((2 * order, RANK), f32),
-            pltpu.VMEM((order, order), f32),
-            pltpu.VMEM((RANK, order), f32),
-            pltpu.VMEM((RANK, order), f32),
+            pltpu.VMEM((2 * ORDER, RANK), f32),
+            pltpu.VMEM((ORDER, ORDER), f32),
+            pltpu.VMEM((RANK, ORDER), f32),
+            pltpu.VMEM((RANK, ORDER), f32),
         ],
         compiler_params=pltpu.CompilerParams(vmem_limit_bytes=32 * 2**20),
-    )(at, *pieces, wide, weights.reshape(1, RANK), place.reshape(-1, 1))
+    )(at, near, far, wide, weights.reshape(1, RANK), place.reshape(-1, 1))
 
 
 def column_kernel(row_ref, user_row_ref, blocks_ref, tiles_ref, out_ref):
@@ -270,83 +251,97 @@
     )(row.reshape(1), user_row.reshape(1, -1), block_ids.T, tiles)
 
 
-def strips(refs, flat_ref):
-    pieces = []
-    for ref in refs:
+def strips(at_ref, refs, flat_ref, users_ref):
+    count = flat_ref.shape[0] // CAP
+    owners = len(refs)
+    for k, ref in enumerate(refs):
         flat_ref[...] = ref[...].astype(f32)
-        count = flat_ref.shape[0] // CAP
         blocks = [flat_ref[pl.ds(b, count, stride=CAP), :] for b in range(CAP)]
-        pieces.append(jnp.concatenate(blocks, axis=1))
-    return jnp.concatenate(pieces, axis=0)
-
-
-def gram_kernel(at_ref, basis_ref, x0_ref, x1_ref, x2_ref, x3_ref, keep_ref, send_ref, flat_ref):
-    x = strips((x0_ref, x1_ref, x2_ref, x3_ref), flat_ref).astype(jnp.bfloat16)
+        owner = lax.rem(at_ref[2] + owners - k, owners)
+        here = pl.ds(pl.multiple_of(owner * count, 16), count)
+        users_ref[here, :] = jnp.concatenate(blocks, axis=1).astype(jnp.bfloat16)
+    return users_ref[...]
+
+
+def gram_kernel(at_ref, basis_ref, x0_ref, x1_ref, x2_ref, x3_ref, keep_ref, send_ref, flat_ref, users_ref, all_ref):
+    x = strips(at_ref, (x0_ref, x1_ref, x2_ref, x3_ref), flat_ref, users_ref)
     parts = split(basis_ref[...])
     high_t, middle_t = (jnp.transpose(p.astype(f32)).astype(jnp.bfloat16) for p in parts[:2])
     one = lambda a, b: jnp.dot(a, b, preferred_element_type=f32)
     both = one(jnp.concatenate([x, high_t], axis=0), jnp.concatenate(parts, axis=1))
     strip = lambda rows, k: both[rows, RANK * k : RANK * (k + 1)]
     users, rest = slice(0, USERS), slice(USERS, None)
-    left = strip(users, 0) + (strip(users, 1) + strip(users, 2))
     small = strip(rest, 1) + strip(rest, 2)
-    own = strip(rest, 0) + (small + jnp.transpose(small) + one(middle_t, parts[1]))
+    all_ref[:RANK, :] = strip(rest, 0) + (small + jnp.transpose(small) + one(middle_t, parts[1]))
+    all_ref[RANK : 3 * RANK, :] = strip(users, 0) + (strip(users, 1) + strip(users, 2))
     cross = lax.dot_general(x, x, (((1,), (1,)), ((), ())), preferred_element_type=f32)
-    low = [own, left[:RANK], left[RANK:]]
-    high = [cross[:RANK, :RANK], cross[:RANK, RANK:], cross[RANK:, RANK:]]
-    half = at_ref[0]
-    for k in range(3):
-        keep_ref[RANK * k : RANK * (k + 1), :] = jnp.where(half == 0, low[k], high[k])
-        send_ref[RANK * k : RANK * (k + 1), :] = jnp.where(half == 0, high[k], low[k])
-
-
-def gram_parts(at, basis, pieces):
+    all_ref[3 * RANK : 4 * RANK, :] = cross[:RANK, :RANK]
+    all_ref[4 * RANK : 5 * RANK, :] = cross[:RANK, RANK:]
+    all_ref[5 * RANK :, :] = cross[RANK:, RANK:]
+    steps, piece = keep_ref.shape[:2]
+    for half, ref in ((at_ref[0], keep_ref), (1 - at_ref[0], send_ref)):
+        for k in range(steps):
+            ring = lax.rem(at_ref[1] + k, steps)
+            first = ((half * steps + ring) * 4 + at_ref[2]) * piece
+            ref[k] = all_ref[pl.ds(pl.multiple_of(first, 8), piece), :]
+
+
+def gram_parts(at, basis, pieces, steps):
     in_vmem = pl.BlockSpec(memory_space=pltpu.VMEM)
+    piece = 6 * RANK // (2 * steps * len(pieces))
     return pl.pallas_call(
         gram_kernel,
-        out_shape=[jax.ShapeDtypeStruct((3 * RANK, RANK), f32)] * 2,
+        out_shape=[jax.ShapeDtypeStruct((steps, piece, RANK), f32)] * 2,
         in_specs=[pl.BlockSpec(memory_space=pltpu.SMEM)] + [in_vmem] * 5,
-        scratch_shapes=[pltpu.VMEM(pieces[0].shape, f32)],
+        scratch_shapes=[
+            pltpu.VMEM(pieces[0].shape, f32),
+            pltpu.VMEM((USERS, basis.shape[0]), jnp.bfloat16),
+            pltpu.VMEM((6 * RANK, RANK), f32),
+        ],
         compiler_params=pltpu.CompilerParams(vmem_limit_bytes=32 * 2**20),
     )(at, basis, *pieces)
 
 
-def wide_kernel(basis_ref, x0_ref, x1_ref, x2_ref, x3_ref, out_ref, flat_ref):
-    out_ref[:, :RANK] = basis_ref[...]
-    out_ref[:, RANK:] = jnp.transpose(strips((x0_ref, x1_ref, x2_ref, x3_ref), flat_ref))
-
-
-def wide_of(basis, pieces):
+def wide_kernel(at_ref, basis_ref, x0_ref, x1_ref, x2_ref, x3_ref, out_ref, flat_ref, users_ref):
+    parts = split(basis_ref[...])
+    x = strips(at_ref, (x0_ref, x1_ref, x2_ref, x3_ref), flat_ref, users_ref)
+    out_ref[:, :RANK] = parts[0]
+    out_ref[:, RANK:ORDER] = jnp.transpose(x.astype(f32)).astype(jnp.bfloat16)
+    out_ref[:, ORDER : ORDER + RANK] = parts[1]
+    out_ref[:, ORDER + RANK :] = parts[2]
+
+
+def wide_of(at, basis, pieces):
     in_vmem = pl.BlockSpec(memory_space=pltpu.VMEM)
     return pl.pallas_call(
         wide_kernel,
-        out_shape=jax.ShapeDtypeStruct((basis.shape[0], RANK + USERS), f32),
-        in_specs=[in_vmem] * 5,
-        scratch_shapes=[pltpu.VMEM(pieces[0].shape, f32)],
+        out_shape=jax.ShapeDtypeStruct((basis.shape[0], ORDER + 2 * RANK), jnp.bfloat16),
+        in_specs=[pl.BlockSpec(memory_space=pltpu.SMEM)] + [in_vmem] * 5,
+        scratch_shapes=[pltpu.VMEM(pieces[0].shape, f32), pltpu.VMEM((USERS, basis.shape[0]), jnp.bfloat16)],
         compiler_params=pltpu.CompilerParams(vmem_limit_bytes=32 * 2**20),
-    )(basis, *pieces)
+    )(at, basis, *pieces)
 
 
 def around(x, axis):
     n = lax.axis_size(axis)
     return [lax.ppermute(x, axis, [(i, (i + k) % n) for i in range(n)]) for k in range(1, n)]
+
+
+def copies(x, axes):
+    x = jnp.broadcast_to(x, (lax.axis_size(axes), *x.shape))
+    return lax.all_to_all(x, axes, split_axis=0, concat_axis=0, tiled=True)
 
 
 def summed(keep, send):
     other = [(0, 1), (1, 0)]
     total = keep + lax.ppermute(send, "item_2", other)
     n = lax.axis_size("item_1")
-    rows = total.shape[0] // n
-    here = lax.axis_index("item_1")
-    part = lambda k: lax.dynamic_slice_in_dim(total, (here + k) % n * rows, rows)
-    own = part(0)
+    own = total[0]
     for k in range(1, n):
-        own = own + lax.ppermute(part(k), "item_1", [(i, (i + k) % n) for i in range(n)])
-    far = lax.axis_size("item_0")
-    every = lax.all_to_all(jnp.broadcast_to(own, (far, *own.shape)), "item_0", 0, 0, tiled=True)
-    own = jnp.sum(every, axis=0)
-    pair = jnp.stack([own, lax.ppermute(own, "item_2", other)])
-    return [pair] + around(pair, "item_1")
+        own = own + lax.ppermute(total[k], "item_1", [(i, (i + k) % n) for i in range(n)])
+    own = jnp.sum(copies(own, "item_0"), axis=0)
+    half = copies(own, ("item_1", "user")).reshape(-1, RANK)
+    return half, lax.ppermute(half, "item_2", other)
 
 
 def per_device(basis, old_values, ratings, block_ids, user_row):
@@ -359,13 +354,13 @@
     arrived = lax.all_to_all(column.reshape(n_item, slab_blocks, width), ITEM, 0, 0, tiled=True)
     arrived = arrived.reshape(n_item * slab_blocks, width)
     pieces = [arrived] + around(arrived, "user")
-    at = jnp.stack([lax.axis_index("item_2"), lax.axis_index("item_1")]).astype(jnp.int32)
-    keep, send = gram_parts(at, basis, pieces)
-    wide = wide_of(basis, pieces)
-    sums = summed(keep, send)
-    steps = (lax.axis_index("user") - user_row % n_user) % n_user
-    place = steps * n_item + user_row // n_user
-    return tuple(core(at, sums, wide, old_values, place, basis.shape[0] * n_item))
+    places = [lax.axis_index(name) for name in ("item_2", "item_1", "user")]
+    at = jnp.stack(places).astype(jnp.int32)
+    keep, send = gram_parts(at, basis, pieces, lax.axis_size("item_1"))
+    wide = wide_of(at, basis, pieces)
+    near, far = summed(keep, send)
+    place = user_row % n_user * n_item + user_row // n_user
+    return tuple(core(at, near, far, wide, old_values, place, basis.shape[0] * n_item))
 
 
 def solution(mesh):

time: 94.2 us -> 91.5 us (0.971)
  waiting for transfers between devices: 18.3 us -> 10.1 us
  blocking collectives: 37.1 us -> 42.7 us
  starting transfers between devices: 13.4 us -> 12 us
  Pallas kernels: 24.1 us -> 25.2 us
    ppermute x6 -> x3, waiting for transfers between devices: 11.9 us -> 5.14 us  [around(): lax.ppermute(x, axis, [(i, (i + k) % n) for i in range(n)])]
    all_to_all x1 -> x2, blocking collectives: 14.1 us -> 19.6 us  [copies(): return lax.all_to_all(x, axes, split_axis=0, concat_axis=0, tiled=True)]
    ppermute x6 -> x3, starting transfers between devices: 5.32 us -> 3.77 us  [around(): lax.ppermute(x, axis, [(i, (i + k) % n) for i in range(n)])]
    ppermute x4, waiting for transfers between devices: 5.32 us -> 4.1 us  [the longest x3 4.05 us: summed(): lax.ppermute(total[k], 'item_1', [(i, (i + k) % n) for i in range(n)])]
  transfers between devices with their start and end apart: 11 -> 8, of which waited for: 10 -> 7; matrix products, arithmetic and copies ran while one was open for 0% -> 0% of each run, Pallas kernels for 0% -> 1%
where the time goes in v2:
time: 91.5 us; the launch traced here: 91.6 us
  blocking collectives  42.7 us (47%)
  Pallas kernels  25.2 us (28%)
  starting transfers between devices  12 us (13%)
  waiting for transfers between devices  10.1 us (11%)
    all_to_all x1, blocking collectives, per_device(): lax.all_to_all(column.reshape(n_item, slab_blocks, width), ITEM, 0, 0, ti...  23.1 us
    pallas_call x1, Pallas kernels, core(): pl.pallas_call(functools.partial(core_kernel, items), out_shape=[jax.Shap...  21.5 us
    all_to_all x2, blocking collectives, copies(): return lax.all_to_all(x, axes, split_axis=0, concat_axis=0, tiled=True)  19.6 us
    ppermute x3, waiting for transfers between devices, around(): lax.ppermute(x, axis, [(i, (i + k) % n) for i in range(n)])  5.14 us
    ppermute x1, starting transfers between devices, summed(): return (half, lax.ppermute(half, 'item_2', other))  4.26 us
    ppermute x3, waiting for transfers between devices, summed(): lax.ppermute(total[k], 'item_1', [(i, (i + k) % n) for i in range(n)])  4.05 us
    ppermute x3, starting transfers between devices, around(): lax.ppermute(x, axis, [(i, (i + k) % n) for i in range(n)])  3.77 us
    ppermute x3, starting transfers between devices, summed(): lax.ppermute(total[k], 'item_1', [(i, (i + k) % n) for i in range(n)])  2.76 us
  transfers between devices with their start and end apart: 8, of which 7 were waited for; matrix products, arithmetic and copies ran while one was open for 0% of the time, Pallas kernels for 1%

profile of v2, /device:TPU:1, one launch (start us, length us, event | category | flops | bytes accessed | tf_op | source)
XLA Modules:
  0.0 91.6 jit_solution(2826820044730560196)
XLA Ops:
  0.6 0.0 copy-start
  0.7 1.8 %shard_map.68 = bf16[256,128]{1,0:T(8,128)(2,1)} custom-call(s32[1]{0:T(128)} %bitcast.3.row_ref, s32[1,256]{1,0:T(1,128)} %bitcast.37, s32[64,256]{1,0:T(8,128)} %bitcast.35, bf16[64,128]{1,0:T(8,128)(2,1)} %bitcast.36), custom_call_target="tpu_custom_call" | custom-call | tf_op jit(solution)/shard_map/pallas_call | solution.py:246
  2.5 23.1 %all_to_all.15 = bf16[64,4,128]{2,1,0:T(4,128)(2,1)S(1)} all-to-all(bf16[64,4,128]{2,1,0:T(4,128)(2,1)} %bitcast.34), channel_id=1, replica_groups=mesh['item_0'=8,'item_1'=4,'item_2'=2,'user'=4] {'item_0','item_1','item..., dimensions={0} | all-to-all | bytes 131072 | tf_op jit(solution)/shard_map/all_to_all | solution.py:354
  25.5 2.7 %collective-permute-start.2 = (bf16[256,128]{1,0:T(8,128)(2,1)S(1)}, bf16[256,128]{1,0:T(8,128)(2,1)S(1)}, u32[]{:S(2)}, u32[]{:S(2)}) collective-permute-start(bf16[256,128]{1,0:T(8,128)(2,1)S(1)} %bitcast.28), channel_id=1, source_target_pairs={{0,3},{1,0},{2,1},{3,2},{4,7},{5,4},{6,5},{7,6},{8,11},{9,8},{10,9... | collective-permute-start | bytes 196616 | tf_op jit(solution)/shard_map/ppermute | solution.py:327
  28.3 0.3 collective-permute-start.1
  28.6 0.7 collective-permute-start
  29.3 0.1 pad_add_fusion.at_ref
  29.4 0.2 collective-permute-done.2.x3_ref
  29.6 3.4 %collective-permute-done.1.x2_ref = bf16[256,128]{1,0:T(8,128)(2,1)S(1)} collective-permute-done((bf16[256,128]{1,0:T(8,128)(2,1)S(1)}, bf16[256,128]{1,0:T(8,128)(2,1)S(1)}, u32[]{:S(2)}, u32[]{:S(2)}) %collective-permute-start.1) | collective-permute-done | bytes 65568 | tf_op jit(solution)/shard_map/ppermute | solution.py:327
  32.9 1.6 %collective-permute-done.x1_ref = bf16[256,128]{1,0:T(8,128)(2,1)S(1)} collective-permute-done((bf16[256,128]{1,0:T(8,128)(2,1)S(1)}, bf16[256,128]{1,0:T(8,128)(2,1)S(1)}, u32[]{:S(2)}, u32[]{:S(2)}) %collective-permute-start) | collective-permute-done | bytes 65568 | tf_op jit(solution)/shard_map/ppermute | solution.py:327
  34.5 0.0 copy-done
  34.5 1.1 %shard_map.69 = (f32[4,24,128]{2,1,0:T(8,128)S(1)}, f32[4,24,128]{2,1,0:T(8,128)S(1)}) custom-call(s32[3]{0:T(128)S(1)} %pad_add_fusion.at_ref, f32[512,128]{1,0:T(8,128)S(1)} %copy-done, bf16[256,128]{1,0:T(8,128)(2,1)S(1)} %bitcast.31, bf16[256,128]{1,0:T(8,128)(2,1)S(1)} %collective-permute-done.x1_ref, ...), custom_call_target="tpu_custom_call" | custom-call | tf_op jit(solution)/shard_map/pallas_call | solution.py:292
  35.7 1.2 %collective-permute-start.3 = (f32[4,24,128]{2,1,0:T(8,128)S(1)}, f32[4,24,128]{2,1,0:T(8,128)S(1)}, u32[]{:S(2)}, u32[]{:S(2)}) collective-permute-start(f32[4,24,128]{2,1,0:T(8,128)S(1)} %get-tuple-element.5), channel_id=1, source_target_pairs={{0,4},{4,0},{1,5},{5,1},{2,6},{6,2},{3,7},{7,3},{8,12},{12,8},{9,1... | collective-permute-start | bytes 147464 | tf_op jit(solution)/shard_map/ppermute | solution.py:337
  36.9 0.9 collective-permute-done.3
  37.8 0.3 collective-permute-start.4
  38.1 2.5 %collective-permute-start.6 = (f32[24,128]{1,0:T(8,128)S(1)}, f32[24,128]{1,0:T(8,128)S(1)}, u32[]{:S(2)}, u32[]{:S(2)}) collective-permute-start(f32[24,128]{1,0:T(8,128)S(1)} %get-tuple-element.7), channel_id=1, source_target_pairs={{0,24},{8,0},{16,8},{24,16},{1,25},{9,1},{17,9},{25,17},{2,26},{10... | collective-permute-start | bytes 36872 | tf_op jit(solution)/shard_map/ppermute | solution.py:341
  40.6 0.0 collective-permute-start.5
  40.6 1.1 %collective-permute-done.4 = f32[24,128]{1,0:T(8,128)S(1)} collective-permute-done((f32[24,128]{1,0:T(8,128)S(1)}, f32[24,128]{1,0:T(8,128)S(1)}, u32[]{:S(2)}, u32[]{:S(2)}) %collective-permute-start.4) | collective-permute-done | bytes 12320 | tf_op jit(solution)/shard_map/ppermute | solution.py:341
  41.6 0.0 collective-permute-done.6
  41.6 3.0 %collective-permute-done.5 = f32[24,128]{1,0:T(8,128)S(1)} collective-permute-done((f32[24,128]{1,0:T(8,128)S(1)}, f32[24,128]{1,0:T(8,128)S(1)}, u32[]{:S(2)}, u32[]{:S(2)}) %collective-permute-start.5) | collective-permute-done | bytes 12320 | tf_op jit(solution)/shard_map/ppermute | solution.py:341
  44.6 10.1 %all_to_all.16 = f32[8,24,128]{2,1,0:T(8,128)S(1)} all-to-all(f32[8,24,128]{2,1,0:T(8,128)S(1)} %broadcast_in_dim.6), channel_id=1, replica_groups=mesh['item_0'=8,'item_1'=4,'item_2'=2,'user'=4] {'item_0'}, dimensions={0} | all-to-all | bytes 196608 | tf_op jit(solution)/shard_map/all_to_all | solution.py:332
  54.7 9.5 %all_to_all.17 = f32[16,24,128]{2,1,0:T(8,128)S(1)} all-to-all(f32[16,24,128]{2,1,0:T(8,128)S(1)} %broadcast_in_dim.7), channel_id=1, replica_groups=mesh['item_0'=8,'item_1'=4,'item_2'=2,'user'=4] {'item_1','user'}, dimensions={0} | all-to-all | bytes 393216 | tf_op jit(solution)/shard_map/all_to_all | solution.py:332
  64.3 0.0 copy-start.2
  64.3 4.3 %collective-permute-start.7 = (f32[384,128]{1,0:T(8,128)S(1)}, f32[384,128]{1,0:T(8,128)S(1)}, u32[]{:S(2)}, u32[]{:S(2)}) collective-permute-start(f32[384,128]{1,0:T(8,128)S(1)} %bitcast.26), channel_id=1, source_target_pairs={{0,4},{4,0},{1,5},{5,1},{2,6},{6,2},{3,7},{7,3},{8,12},{12,8},{9,1... | collective-permute-start | bytes 589832 | tf_op jit(solution)/shard_map/ppermute | solution.py:344
  68.5 0.0 copy-done.2
  68.5 0.1 copy.8.place_ref
  68.7 0.8 shard_map.70.wide_ref
  69.5 0.0 copy-start.1
  69.5 0.1 collective-permute-done.7.far_ref
  69.6 0.6 copy-done.1
  70.2 21.5 %shard_map.71 = (f32[512,128]{1,0:T(8,128)}, f32[256,128]{1,0:T(8,128)}) custom-call(s32[3]{0:T(128)S(1)} %pad_add_fusion.at_ref, f32[384,128]{1,0:T(8,128)S(1)} %bitcast.27, f32[384,128]{1,0:T(8,128)S(1)} %collective-permute-done.7.far_ref, bf16[512,640]{1,0:T(8,128)(2,1)S(1)} %shard_map.70.wide_ref, f32[1,128]{1,0:T(1,128)S(1)} %bitcast.33, ...), custom_call_target="tpu_custom_call" | custom-call | tf_op jit(solution)/shard_map/pallas_call | solution.py:220
  (7 shorter events, 0.1 us)
Async XLA Ops:
  0.6 33.9 %copy-start = (f32[512,128]{1,0:T(8,128)S(1)}, f32[512,128]{1,0:T(8,128)}, u32[]{:S(2)}) copy-start(f32[512,128]{1,0:T(8,128)} %basis_ref.3) | copy-start | bytes 786436
  25.5 4.1 %collective-permute-start.2 = (bf16[256,128]{1,0:T(8,128)(2,1)S(1)}, bf16[256,128]{1,0:T(8,128)(2,1)S(1)}, u32[]{:S(2)}, u32[]{:S(2)}) collective-permute-start(bf16[256,128]{1,0:T(8,128)(2,1)S(1)} %bitcast.28), channel_id=1, source_target_pairs={{0,3},{1,0},{2,1},{3,2},{4,7},{5,4},{6,5},{7,6},{8,11},{9,8},{10,9... | collective-permute-start | bytes 196616 | tf_op jit(solution)/shard_map/ppermute | solution.py:327
  28.3 4.7 %collective-permute-start.1 = (bf16[256,128]{1,0:T(8,128)(2,1)S(1)}, bf16[256,128]{1,0:T(8,128)(2,1)S(1)}, u32[]{:S(2)}, u32[]{:S(2)}) collective-permute-start(bf16[256,128]{1,0:T(8,128)(2,1)S(1)} %bitcast.29), channel_id=1, source_target_pairs={{0,2},{1,3},{2,0},{3,1},{4,6},{5,7},{6,4},{7,5},{8,10},{9,11},{10,... | collective-permute-start | bytes 196616 | tf_op jit(solution)/shard_map/ppermute | solution.py:327
  28.6 5.9 %collective-permute-start = (bf16[256,128]{1,0:T(8,128)(2,1)S(1)}, bf16[256,128]{1,0:T(8,128)(2,1)S(1)}, u32[]{:S(2)}, u32[]{:S(2)}) collective-permute-start(bf16[256,128]{1,0:T(8,128)(2,1)S(1)} %bitcast.30), channel_id=1, source_target_pairs={{0,1},{1,2},{2,3},{3,0},{4,5},{5,6},{6,7},{7,4},{8,9},{9,10},{10,1... | collective-permute-start | bytes 196616 | tf_op jit(solution)/shard_map/ppermute | solution.py:327
  35.7 2.1 %collective-permute-start.3 = (f32[4,24,128]{2,1,0:T(8,128)S(1)}, f32[4,24,128]{2,1,0:T(8,128)S(1)}, u32[]{:S(2)}, u32[]{:S(2)}) collective-permute-start(f32[4,24,128]{2,1,0:T(8,128)S(1)} %get-tuple-element.5), channel_id=1, source_target_pairs={{0,4},{4,0},{1,5},{5,1},{2,6},{6,2},{3,7},{7,3},{8,12},{12,8},{9,1... | collective-permute-start | bytes 147464 | tf_op jit(solution)/shard_map/ppermute | solution.py:337
  37.8 3.8 %collective-permute-start.4 = (f32[24,128]{1,0:T(8,128)S(1)}, f32[24,128]{1,0:T(8,128)S(1)}, u32[]{:S(2)}, u32[]{:S(2)}) collective-permute-start(f32[24,128]{1,0:T(8,128)S(1)} %get-tuple-element.6), channel_id=1, source_target_pairs={{0,8},{8,16},{16,24},{24,0},{1,9},{9,17},{17,25},{25,1},{2,10},{10... | collective-permute-start | bytes 36872 | tf_op jit(solution)/shard_map/ppermute | solution.py:341
  38.1 3.6 %collective-permute-start.6 = (f32[24,128]{1,0:T(8,128)S(1)}, f32[24,128]{1,0:T(8,128)S(1)}, u32[]{:S(2)}, u32[]{:S(2)}) collective-permute-start(f32[24,128]{1,0:T(8,128)S(1)} %get-tuple-element.7), channel_id=1, source_target_pairs={{0,24},{8,0},{16,8},{24,16},{1,25},{9,1},{17,9},{25,17},{2,26},{10... | collective-permute-start | bytes 36872 | tf_op jit(solution)/shard_map/ppermute | solution.py:341
  40.6 4.0 %collective-permute-start.5 = (f32[24,128]{1,0:T(8,128)S(1)}, f32[24,128]{1,0:T(8,128)S(1)}, u32[]{:S(2)}, u32[]{:S(2)}) collective-permute-start(f32[24,128]{1,0:T(8,128)S(1)} %get-tuple-element.8), channel_id=1, source_target_pairs={{0,16},{8,24},{16,0},{24,8},{1,17},{9,25},{17,1},{25,9},{2,18},{10... | collective-permute-start | bytes 36872 | tf_op jit(solution)/shard_map/ppermute | solution.py:341
  64.3 4.3 %copy-start.2 = (s32[256]{0:T(256)S(1)}, s32[256]{0:T(256)}, u32[]{:S(2)}) copy-start(s32[256]{0:T(256)} %param.9) | copy-start | bytes 3076
  64.3 5.3 %collective-permute-start.7 = (f32[384,128]{1,0:T(8,128)S(1)}, f32[384,128]{1,0:T(8,128)S(1)}, u32[]{:S(2)}, u32[]{:S(2)}) collective-permute-start(f32[384,128]{1,0:T(8,128)S(1)} %bitcast.26), channel_id=1, source_target_pairs={{0,4},{4,0},{1,5},{5,1},{2,6},{6,2},{3,7},{7,3},{8,12},{12,8},{9,1... | collective-permute-start | bytes 589832 | tf_op jit(solution)/shard_map/ppermute | solution.py:344
  69.5 0.7 copy-start.1

commit v3 on v2

--- a/solution.py
+++ b/solution.py
@@ -125,7 +125,9 @@
     i, k = square_iotas()
     off = mm_nt(x, y) - jnp.where(i == k, 1.0, 0.0)
     step = jnp.where(i > k, off, jnp.where(i == k, 0.5 * off, 0.0))
-    return x - mm(step, x), y - mm(step, y)
+    both = jnp.concatenate([x, y], axis=1)
+    both = both - jnp.dot(step.astype(jnp.bfloat16), both.astype(jnp.bfloat16), preferred_element_type=f32)
+    return both[:, :ORDER], both[:, ORDER:]
 
 
 def assemble(sums, weights, items):
@@ -148,13 +150,8 @@
 
 
 def core_kernel(
-    items, at_ref, near_ref, far_ref, wide_ref, weights_ref, place_ref,
-    rows_ref, factors_ref, sums_ref, gram_ref, turn_t_ref, back_ref,
+    items, sums_ref, wide_ref, weights_ref, place_ref, rows_ref, factors_ref, gram_ref, turn_t_ref, back_ref
 ):
-    piece = near_ref.shape[0]
-    for k, ref in enumerate((near_ref, far_ref)):
-        first = piece * (at_ref[0] if k == 0 else 1 - at_ref[0])
-        sums_ref[pl.ds(pl.multiple_of(first, 8), piece), :] = ref[...]
     weights = weights_ref[...]
     whole, size = assemble(sums_ref, weights, items)
     gram_ref[...] = whole
@@ -166,18 +163,18 @@
     low1, piv1 = eliminate(h1)
     x = turned(low1, piv1, x)
     x = mm(x, g)
-    y = mm(x, g)
-    h2 = mm_nt(x, y)
+    part = split(x)
+    h2 = mm_nt(part, part)
     low2, piv2 = eliminate(h2)
-    x = turned(low2, piv2, y)
+    x = turned(low2, piv2, x)
+    x = mm(x, g)
     x = mm(x, g)
     y = mm(x, g)
     h3 = mm_nt(x, y)
     low3, piv3 = eliminate(h3)
     turn_t_ref[...] = turned(low3, piv3, x)
     back_ref[...] = turned(low3, piv3, y)
-    last = smallest(piv3, h3)
-    fine = (smallest(piv1, h1) > 3e-5) & (smallest(piv2, h2) > 1e-5) & (last > 1e-4)
+    fine = (smallest(piv1, h1) > 3e-5) & (smallest(piv2, h2) > 1e-4) & (smallest(piv3, h3) > 5e-5)
 
     @pl.when(jnp.logical_not(fine))
     def _():
@@ -195,14 +192,9 @@
         )
         lax.fori_loop(0, 9, turn, start)
 
-    @pl.when(jnp.logical_not(fine & (last > 2e-2)))
-    def _():
-        x, y = polished(turn_t_ref[...], back_ref[...])
-        turn_t_ref[...] = x
-        back_ref[...] = y
-
+    x, y = polished(turn_t_ref[...], back_ref[...])
     scale = lax.rsqrt(size)
-    x = turn_t_ref[...] * scale
+    x = x * scale
     left = split(jnp.concatenate([x[:, :RANK] * weights, x[:, RANK:]], axis=1))
     one = lambda a, b: lax.dot_general(a, b, (((1,), (1,)), ((), ())), preferred_element_type=f32)
     most = one(wide_ref[:, :ORDER], jnp.concatenate(left, axis=0))
@@ -210,45 +202,53 @@
     least = one(wide_ref[:, ORDER + RANK :], left[0][:, :RANK])
     strip = lambda y, k: y[:, RANK * k : RANK * (k + 1)]
     rows_ref[...] = strip(most, 0) + ((strip(most, 1) + strip(some, 0)) + (strip(most, 2) + strip(some, 1) + least))
-    user_of = place_ref[...]
-    onehot = jnp.where(lax.broadcasted_iota(jnp.int32, (USERS, USERS), 1) == user_of, 1.0, 0.0)
-    factors_ref[...] = mm_nt(onehot, back_ref[:, RANK:] * (scale * size))
-
-
-def core(at, near, far, wide, weights, place, items):
+    taken = lax.broadcasted_iota(jnp.int32, (USERS, USERS), 0) == place_ref[...]
+    taken = jnp.where(taken, 1.0, 0.0).astype(jnp.bfloat16)
+    parts = jnp.concatenate(split(y[:, RANK:] * (scale * size)), axis=0)
+    found = jnp.dot(parts, taken, preferred_element_type=f32)
+    found = found[:RANK] + (found[RANK : 2 * RANK] + found[2 * RANK :])
+    factors_ref[...] = jnp.transpose(found)
+
+
+def core(sums, wide, weights, place, items):
     in_vmem = pl.BlockSpec(memory_space=pltpu.VMEM)
     return pl.pallas_call(
         functools.partial(core_kernel, items),
         out_shape=[jax.ShapeDtypeStruct((wide.shape[0], RANK), f32), jax.ShapeDtypeStruct((USERS, RANK), f32)],
-        in_specs=[pl.BlockSpec(memory_space=pltpu.SMEM)] + [in_vmem] * 5,
+        in_specs=[in_vmem] * 4,
         scratch_shapes=[
-            pltpu.VMEM((2 * ORDER, RANK), f32),
             pltpu.VMEM((ORDER, ORDER), f32),
             pltpu.VMEM((RANK, ORDER), f32),
             pltpu.VMEM((RANK, ORDER), f32),
         ],
         compiler_params=pltpu.CompilerParams(vmem_limit_bytes=32 * 2**20),
-    )(at, near, far, wide, weights.reshape(1, RANK), place.reshape(-1, 1))
-
-
-def column_kernel(row_ref, user_row_ref, blocks_ref, tiles_ref, out_ref):
-    mine = user_row_ref[...] == row_ref[0]
+    )(sums, wide, weights, place)
+
+
+def column_kernel(n_user, row_ref, user_row_ref, blocks_ref, tiles_ref, weights_ref, out_ref, place_ref, same_ref):
+    user_row = user_row_ref[...]
+    mine = user_row == row_ref[0]
     blocks = jnp.sum(jnp.where(mine, blocks_ref[...], 0), axis=1, keepdims=True)
     count = out_ref.shape[0]
     place = lax.broadcasted_iota(jnp.int32, (blocks.shape[0], count), 1) == blocks
     place = jnp.where(place, 1.0, 0.0).astype(jnp.bfloat16)
     dense = lax.dot_general(place, tiles_ref[...], (((0,), (0,)), ((), ())), preferred_element_type=f32)
     out_ref[...] = dense.astype(jnp.bfloat16)
-
-
-def column_of(row, user_row, block_ids, tiles, count):
+    place_ref[...] = lax.rem(user_row, n_user) * (user_row.shape[1] // n_user) + lax.div(user_row, n_user)
+    same_ref[...] = weights_ref[...]
+
+
+def column_of(row, user_row, block_ids, tiles, weights, count, n_user):
     in_vmem = pl.BlockSpec(memory_space=pltpu.VMEM)
     return pl.pallas_call(
-        column_kernel,
-        out_shape=jax.ShapeDtypeStruct((count, tiles.shape[1]), jnp.bfloat16),
-        in_specs=[pl.BlockSpec(memory_space=pltpu.SMEM), in_vmem, in_vmem, in_vmem],
-        out_specs=in_vmem,
-    )(row.reshape(1), user_row.reshape(1, -1), block_ids.T, tiles)
+        functools.partial(column_kernel, n_user),
+        out_shape=[
+            jax.ShapeDtypeStruct((count, tiles.shape[1]), jnp.bfloat16),
+            jax.ShapeDtypeStruct((1, user_row.shape[0]), jnp.int32),
+            jax.ShapeDtypeStruct((1, weights.shape[0]), f32),
+        ],
+        in_specs=[pl.BlockSpec(memory_space=pltpu.SMEM)] + [in_vmem] * 4,
+    )(row.reshape(1), user_row.reshape(1, -1), block_ids.T, tiles, weights.reshape(1, -1))
 
 
 def strips(at_ref, refs, flat_ref, users_ref):
@@ -257,13 +257,13 @@
     for k, ref in enumerate(refs):
         flat_ref[...] = ref[...].astype(f32)
         blocks = [flat_ref[pl.ds(b, count, stride=CAP), :] for b in range(CAP)]
-        owner = lax.rem(at_ref[2] + owners - k, owners)
+        owner = lax.rem(at_ref[0] + owners - k, owners)
         here = pl.ds(pl.multiple_of(owner * count, 16), count)
         users_ref[here, :] = jnp.concatenate(blocks, axis=1).astype(jnp.bfloat16)
     return users_ref[...]
 
 
-def gram_kernel(at_ref, basis_ref, x0_ref, x1_ref, x2_ref, x3_ref, keep_ref, send_ref, flat_ref, users_ref, all_ref):
+def gram_kernel(at_ref, basis_ref, x0_ref, x1_ref, x2_ref, x3_ref, out_ref, flat_ref, users_ref, all_ref):
     x = strips(at_ref, (x0_ref, x1_ref, x2_ref, x3_ref), flat_ref, users_ref)
     parts = split(basis_ref[...])
     high_t, middle_t = (jnp.transpose(p.astype(f32)).astype(jnp.bfloat16) for p in parts[:2])
@@ -278,20 +278,17 @@
     all_ref[3 * RANK : 4 * RANK, :] = cross[:RANK, :RANK]
     all_ref[4 * RANK : 5 * RANK, :] = cross[:RANK, RANK:]
     all_ref[5 * RANK :, :] = cross[RANK:, RANK:]
-    steps, piece = keep_ref.shape[:2]
-    for half, ref in ((at_ref[0], keep_ref), (1 - at_ref[0], send_ref)):
-        for k in range(steps):
-            ring = lax.rem(at_ref[1] + k, steps)
-            first = ((half * steps + ring) * 4 + at_ref[2]) * piece
-            ref[k] = all_ref[pl.ds(pl.multiple_of(first, 8), piece), :]
-
-
-def gram_parts(at, basis, pieces, steps):
+    count, piece = out_ref.shape[:2]
+    for k in range(count):
+        first = (k * 4 + at_ref[0]) * piece
+        out_ref[k] = all_ref[pl.ds(pl.multiple_of(first, 8), piece), :]
+
+
+def gram_parts(at, basis, pieces, count):
     in_vmem = pl.BlockSpec(memory_space=pltpu.VMEM)
-    piece = 6 * RANK // (2 * steps * len(pieces))
     return pl.pallas_call(
         gram_kernel,
-        out_shape=[jax.ShapeDtypeStruct((steps, piece, RANK), f32)] * 2,
+        out_shape=jax.ShapeDtypeStruct((count, 6 * RANK // (count * len(pieces)), RANK), f32),
         in_specs=[pl.BlockSpec(memory_space=pltpu.SMEM)] + [in_vmem] * 5,
         scratch_shapes=[
             pltpu.VMEM(pieces[0].shape, f32),
@@ -332,16 +329,11 @@
     return lax.all_to_all(x, axes, split_axis=0, concat_axis=0, tiled=True)
 
 
-def summed(keep, send):
-    other = [(0, 1), (1, 0)]
-    total = keep + lax.ppermute(send, "item_2", other)
-    n = lax.axis_size("item_1")
-    own = total[0]
-    for k in range(1, n):
-        own = own + lax.ppermute(total[k], "item_1", [(i, (i + k) % n) for i in range(n)])
+def summed(parts):
+    near = ("item_1", "item_2")
+    own = jnp.sum(lax.all_to_all(parts, near, 0, 0, tiled=True), axis=0)
     own = jnp.sum(copies(own, "item_0"), axis=0)
-    half = copies(own, ("item_1", "user")).reshape(-1, RANK)
-    return half, lax.ppermute(half, "item_2", other)
+    return copies(own, (*near, "user")).reshape(-1, RANK)
 
 
 def per_device(basis, old_values, ratings, block_ids, user_row):
@@ -349,18 +341,16 @@
     n_user = lax.axis_size("user")
     width = ratings.shape[2]
     slab_blocks = basis.shape[0] // width
-    row = lax.axis_index(ITEM) * n_user + lax.axis_index("user")
-    column = column_of(row, user_row, block_ids, ratings[0], n_item * slab_blocks)
+    user = lax.axis_index("user")
+    row = lax.axis_index(ITEM) * n_user + user
+    at = user.reshape(1)
+    column, place, weights = column_of(row, user_row, block_ids, ratings[0], old_values, n_item * slab_blocks, n_user)
     arrived = lax.all_to_all(column.reshape(n_item, slab_blocks, width), ITEM, 0, 0, tiled=True)
     arrived = arrived.reshape(n_item * slab_blocks, width)
     pieces = [arrived] + around(arrived, "user")
-    places = [lax.axis_index(name) for name in ("item_2", "item_1", "user")]
-    at = jnp.stack(places).astype(jnp.int32)
-    keep, send = gram_parts(at, basis, pieces, lax.axis_size("item_1"))
+    parts = gram_parts(at, basis, pieces, lax.axis_size("item_1") * lax.axis_size("item_2"))
     wide = wide_of(at, basis, pieces)
-    near, far = summed(keep, send)
-    place = user_row % n_user * n_item + user_row // n_user
-    return tuple(core(at, near, far, wide, old_values, place, basis.shape[0] * n_item))
+    return tuple(core(summed(parts), wide, weights, place, basis.shape[0] * n_item))
 
 
 def solution(mesh):

time: 91.5 us -> 91.6 us (level)
  waiting for transfers between devices: 10.1 us -> 14.8 us
  starting transfers between devices: 12 us -> 9.6 us
  Pallas kernels: 25.2 us -> 23.2 us
  blocking collectives: 42.7 us -> 41.4 us
    all_to_all x2 -> x1, blocking collectives: 19.6 us -> 9.83 us  [copies(): return lax.all_to_all(x, axes, split_axis=0, concat_axis=0, tiled=True)]
    all_to_all x0 -> x1, waiting for transfers between devices: none -> 9.63 us  [copies(): return lax.all_to_all(x, axes, split_axis=0, concat_axis=0, tiled=True)]
    all_to_all x0 -> x1, blocking collectives: none -> 8.52 us  [summed(): own = jnp.sum(lax.all_to_all(parts, near, 0, 0, tiled=True), axis=0)]
    ppermute x5 -> x0, starting transfers between devices: 8.27 us -> none  [the longest x1 4.26 us: summed(): return (half, lax.ppermute(half, 'item_2', other))]
    all_to_all x0 -> x1, starting transfers between devices: none -> 5.83 us  [copies(): return lax.all_to_all(x, axes, split_axis=0, concat_axis=0, tiled=True)]
    ppermute x5 -> x0, waiting for transfers between devices: 4.98 us -> none  [the longest x3 4.05 us: summed(): lax.ppermute(total[k], 'item_1', [(i, (i + k) % n) for i in range(n)])]
    pallas_call x1, Pallas kernels: 21.5 us -> 20.5 us  [core(): pl.pallas_call(functools.partial(core_kernel, items), out_shape=[jax.Shap...]
  transfers between devices with their start and end apart: 8 -> 4, of which waited for: 7 -> 4; matrix products, arithmetic and copies ran while one was open for 0% -> 0% of each run, Pallas kernels for 1% -> 0%
where the time goes in v3:
time: 91.6 us; the launch traced here: 91.3 us
  blocking collectives  41.4 us (45%)
  Pallas kernels  23.2 us (25%)
  waiting for transfers between devices  14.8 us (16%)
  starting transfers between devices  9.6 us (10%)
  local copies, waits for them, and re-layouts  1.49 us (2%)
    all_to_all x1, blocking collectives, per_device(): lax.all_to_all(column.reshape(n_item, slab_blocks, width), ITEM, 0, 0, ti...  23.1 us
    pallas_call x1, Pallas kernels, core(): pl.pallas_call(functools.partial(core_kernel, items), out_shape=[jax.Shap...  20.5 us
    all_to_all x1, blocking collectives, copies(): return lax.all_to_all(x, axes, split_axis=0, concat_axis=0, tiled=True)  9.83 us
    all_to_all x1, waiting for transfers between devices, copies(): return lax.all_to_all(x, axes, split_axis=0, concat_axis=0, tiled=True)  9.63 us
    all_to_all x1, blocking collectives, summed(): own = jnp.sum(lax.all_to_all(parts, near, 0, 0, tiled=True), axis=0)  8.52 us
    all_to_all x1, starting transfers between devices, copies(): return lax.all_to_all(x, axes, split_axis=0, concat_axis=0, tiled=True)  5.83 us
    ppermute x3, waiting for transfers between devices, around(): lax.ppermute(x, axis, [(i, (i + k) % n) for i in range(n)])  5.21 us
    ppermute x3, starting transfers between devices, around(): lax.ppermute(x, axis, [(i, (i + k) % n) for i in range(n)])  3.78 us
  transfers between devices with their start and end apart: 4, of which 4 were waited for; matrix products, arithmetic and copies ran while one was open for 0% of the time, Pallas kernels for 0%

profile of v3, /device:TPU:1, one launch (start us, length us, event | category | flops | bytes accessed | tf_op | source)
XLA Modules:
  0.0 91.3 jit_solution(7412450806830213799)
XLA Ops:
  0.6 0.0 copy-start
  0.7 1.8 %shard_map.68 = (bf16[256,128]{1,0:T(8,128)(2,1)}, s32[1,256]{1,0:T(1,128)}, f32[1,128]{1,0:T(1,128)}) custom-call(s32[1]{0:T(128)} %bitcast.1.row_ref, s32[1,256]{1,0:T(1,128)} %bitcast.18, s32[64,256]{1,0:T(8,128)} %bitcast.15, bf16[64,128]{1,0:T(8,128)(2,1)} %bitcast.17, f32[1,128]{1,0:T(1,128)} %bitcast.19), custom_call_target="tpu_custom_call" | custom-call | tf_op jit(solution)/shard_map/pallas_call | solution.py:243
  2.5 23.1 %all_to_all.20 = bf16[64,4,128]{2,1,0:T(4,128)(2,1)S(1)} all-to-all(bf16[64,4,128]{2,1,0:T(4,128)(2,1)} %bitcast.16), channel_id=1, replica_groups=mesh['item_0'=8,'item_1'=4,'item_2'=2,'user'=4] {'item_0','item_1','item..., dimensions={0} | all-to-all | bytes 131072 | tf_op jit(solution)/shard_map/all_to_all | solution.py:348
  25.5 2.7 %collective-permute-start.2 = (bf16[256,128]{1,0:T(8,128)(2,1)S(1)}, bf16[256,128]{1,0:T(8,128)(2,1)S(1)}, u32[]{:S(2)}, u32[]{:S(2)}) collective-permute-start(bf16[256,128]{1,0:T(8,128)(2,1)S(1)} %bitcast.10), channel_id=1, source_target_pairs={{0,3},{1,0},{2,1},{3,2},{4,7},{5,4},{6,5},{7,6},{8,11},{9,8},{10,9... | collective-permute-start | bytes 196616 | tf_op jit(solution)/shard_map/ppermute | solution.py:324
  28.3 0.3 collective-permute-start.1
  28.6 0.7 collective-permute-start
  29.3 0.3 collective-permute-done.2.x3_ref
  29.6 3.4 %collective-permute-done.1.x2_ref = bf16[256,128]{1,0:T(8,128)(2,1)S(1)} collective-permute-done((bf16[256,128]{1,0:T(8,128)(2,1)S(1)}, bf16[256,128]{1,0:T(8,128)(2,1)S(1)}, u32[]{:S(2)}, u32[]{:S(2)}) %collective-permute-start.1) | collective-permute-done | bytes 65568 | tf_op jit(solution)/shard_map/ppermute | solution.py:324
  33.0 1.6 %collective-permute-done.x1_ref = bf16[256,128]{1,0:T(8,128)(2,1)S(1)} collective-permute-done((bf16[256,128]{1,0:T(8,128)(2,1)S(1)}, bf16[256,128]{1,0:T(8,128)(2,1)S(1)}, u32[]{:S(2)}, u32[]{:S(2)}) %collective-permute-start) | collective-permute-done | bytes 65568 | tf_op jit(solution)/shard_map/ppermute | solution.py:324
  34.5 0.0 copy-done
  34.5 0.6 shard_map.69
  35.1 8.5 %all_to_all.21 = f32[8,24,128]{2,1,0:T(8,128)S(1)} all-to-all(f32[8,24,128]{2,1,0:T(8,128)S(1)} %shard_map.69), channel_id=1, replica_groups=mesh['item_0'=8,'item_1'=4,'item_2'=2,'user'=4] {'item_1','item_2'}, dimensions={0} | all-to-all | bytes 196608 | tf_op jit(solution)/shard_map/all_to_all | solution.py:334
  43.7 9.8 %all_to_all.22 = f32[8,24,128]{2,1,0:T(8,128)S(1)} all-to-all(f32[8,24,128]{2,1,0:T(8,128)S(1)} %broadcast_in_dim.6), channel_id=1, replica_groups=mesh['item_0'=8,'item_1'=4,'item_2'=2,'user'=4] {'item_0'}, dimensions={0} | all-to-all | bytes 196608 | tf_op jit(solution)/shard_map/all_to_all | solution.py:329
  53.5 0.8 broadcast_in_dim.7
  54.3 5.8 %all-to-all-start.3 = ((f32[32,24,128]{2,1,0:T(8,128)}), f32[32,24,128]{2,1,0:T(8,128)S(1)}, u32[]{:S(2)}, u32[]{:S(2)}) async-start(f32[32,24,128]{2,1,0:T(8,128)} %broadcast_in_dim.7), calls=%async_computation.3 | async-start | bytes 786432 | tf_op jit(solution)/shard_map/all_to_all | solution.py:329
  60.1 0.3 shard_map.70.wide_ref
  60.5 9.6 %all-to-all-done.3 = f32[32,24,128]{2,1,0:T(8,128)S(1)} async-done(((f32[32,24,128]{2,1,0:T(8,128)}), f32[32,24,128]{2,1,0:T(8,128)S(1)}, u32[]{:S(2)}, u32[]{:S(2)}) %all-to-all-start.3) | async-done | bytes 393248 | tf_op jit(solution)/shard_map/all_to_all | solution.py:329
  70.1 0.0 copy-start.1
  70.1 0.0 copy-start.2
  70.1 0.7 copy-done.1
  70.8 0.0 copy-done.2
  70.8 20.5 %shard_map.71 = (f32[512,128]{1,0:T(8,128)}, f32[256,128]{1,0:T(8,128)}) custom-call(f32[768,128]{1,0:T(8,128)S(1)} %bitcast.9, bf16[512,640]{1,0:T(8,128)(2,1)S(1)} %shard_map.70.wide_ref, f32[1,128]{1,0:T(1,128)S(1)} %copy-done.2, s32[1,256]{1,0:T(1,128)S(1)} %copy-done.1), custom_call_target="tpu_custom_call" | custom-call | tf_op jit(solution)/shard_map/pallas_call | solution.py:215
  (3 shorter events, 0.0 us)
Async XLA Ops:
  0.6 33.9 %copy-start = (f32[512,128]{1,0:T(8,128)S(1)}, f32[512,128]{1,0:T(8,128)}, u32[]{:S(2)}) copy-start(f32[512,128]{1,0:T(8,128)} %basis_ref.3) | copy-start | bytes 786436
  25.5 4.1 %collective-permute-start.2 = (bf16[256,128]{1,0:T(8,128)(2,1)S(1)}, bf16[256,128]{1,0:T(8,128)(2,1)S(1)}, u32[]{:S(2)}, u32[]{:S(2)}) collective-permute-start(bf16[256,128]{1,0:T(8,128)(2,1)S(1)} %bitcast.10), channel_id=1, source_target_pairs={{0,3},{1,0},{2,1},{3,2},{4,7},{5,4},{6,5},{7,6},{8,11},{9,8},{10,9... | collective-permute-start | bytes 196616 | tf_op jit(solution)/shard_map/ppermute | solution.py:324
  28.3 4.7 %collective-permute-start.1 = (bf16[256,128]{1,0:T(8,128)(2,1)S(1)}, bf16[256,128]{1,0:T(8,128)(2,1)S(1)}, u32[]{:S(2)}, u32[]{:S(2)}) collective-permute-start(bf16[256,128]{1,0:T(8,128)(2,1)S(1)} %bitcast.11), channel_id=1, source_target_pairs={{0,2},{1,3},{2,0},{3,1},{4,6},{5,7},{6,4},{7,5},{8,10},{9,11},{10,... | collective-permute-start | bytes 196616 | tf_op jit(solution)/shard_map/ppermute | solution.py:324
  28.6 5.9 %collective-permute-start = (bf16[256,128]{1,0:T(8,128)(2,1)S(1)}, bf16[256,128]{1,0:T(8,128)(2,1)S(1)}, u32[]{:S(2)}, u32[]{:S(2)}) collective-permute-start(bf16[256,128]{1,0:T(8,128)(2,1)S(1)} %bitcast.12), channel_id=1, source_target_pairs={{0,1},{1,2},{2,3},{3,0},{4,5},{5,6},{6,7},{7,4},{8,9},{9,10},{10,1... | collective-permute-start | bytes 196616 | tf_op jit(solution)/shard_map/ppermute | solution.py:324
  54.3 15.8 %all-to-all-start.3 = ((f32[32,24,128]{2,1,0:T(8,128)}), f32[32,24,128]{2,1,0:T(8,128)S(1)}, u32[]{:S(2)}, u32[]{:S(2)}) async-start(f32[32,24,128]{2,1,0:T(8,128)} %broadcast_in_dim.7), calls=%async_computation.3 | async-start | bytes 786432 | tf_op jit(solution)/shard_map/all_to_all | solution.py:329
  70.1 0.7 copy-start.1
  70.1 0.7 copy-start.2

commit v4 on v3

--- a/solution.py
+++ b/solution.py
@@ -83,7 +83,7 @@
                 column[k] = column[k] - one * upper[k - s] - two * under[k - s - 1]
         rows[panel] = here
         pivots.append(pivot_of_row)
-        for other in range(panel + 1, count):
+        for other in range(panel + 1, min(panel + 2, count)):
             there = rows[other]
             column = [spread(there[:, first + k : first + k + 1]) for k in range(8)]
             for s, (inverse, line, upper) in enumerate(steps):
@@ -91,6 +91,17 @@
                 there = there - factor * line
                 for k in range(s + 1, 8):
                     column[k] = column[k] - factor * upper[k - s]
+            rows[other] = there
+        solved = [None] * 8
+        for s in range(7, -1, -1):
+            inverse, line, upper = steps[s]
+            for k in range(s + 1, 8):
+                line = line - upper[k - s] * solved[k]
+            solved[s] = line * inverse
+        for other in range(panel + 2, count):
+            there = rows[other]
+            for k in range(8):
+                there = there - spread(rows[other][:, first + k : first + k + 1]) * solved[k]
             rows[other] = there
     return lower_of(jnp.concatenate(rows, axis=0)), jnp.concatenate(pivots, axis=0)
 
@@ -150,8 +161,12 @@
 
 
 def core_kernel(
-    items, sums_ref, wide_ref, weights_ref, place_ref, rows_ref, factors_ref, gram_ref, turn_t_ref, back_ref
+    items, at_ref, near_ref, far_ref, wide_ref, weights_ref, place_ref,
+    rows_ref, factors_ref, sums_ref, gram_ref, turn_t_ref, back_ref,
 ):
+    half = near_ref.shape[0]
+    for place, ref in ((at_ref[1], near_ref), (1 - at_ref[1], far_ref)):
+        sums_ref[pl.ds(pl.multiple_of(place * half, 8), half), :] = ref[...]
     weights = weights_ref[...]
     whole, size = assemble(sums_ref, weights, items)
     gram_ref[...] = whole
@@ -210,45 +225,39 @@
     factors_ref[...] = jnp.transpose(found)
 
 
-def core(sums, wide, weights, place, items):
+def core(at, near, far, wide, weights, place, items):
     in_vmem = pl.BlockSpec(memory_space=pltpu.VMEM)
     return pl.pallas_call(
         functools.partial(core_kernel, items),
         out_shape=[jax.ShapeDtypeStruct((wide.shape[0], RANK), f32), jax.ShapeDtypeStruct((USERS, RANK), f32)],
-        in_specs=[in_vmem] * 4,
+        in_specs=[pl.BlockSpec(memory_space=pltpu.SMEM)] + [in_vmem] * 5,
         scratch_shapes=[
+            pltpu.VMEM((2 * ORDER, RANK), f32),
             pltpu.VMEM((ORDER, ORDER), f32),
             pltpu.VMEM((RANK, ORDER), f32),
             pltpu.VMEM((RANK, ORDER), f32),
         ],
         compiler_params=pltpu.CompilerParams(vmem_limit_bytes=32 * 2**20),
-    )(sums, wide, weights, place)
-
-
-def column_kernel(n_user, row_ref, user_row_ref, blocks_ref, tiles_ref, weights_ref, out_ref, place_ref, same_ref):
-    user_row = user_row_ref[...]
-    mine = user_row == row_ref[0]
+    )(at, near, far, wide, weights, place)
+
+
+def column_kernel(row_ref, user_row_ref, blocks_ref, tiles_ref, out_ref):
+    mine = user_row_ref[...] == row_ref[0]
     blocks = jnp.sum(jnp.where(mine, blocks_ref[...], 0), axis=1, keepdims=True)
     count = out_ref.shape[0]
     place = lax.broadcasted_iota(jnp.int32, (blocks.shape[0], count), 1) == blocks
     place = jnp.where(place, 1.0, 0.0).astype(jnp.bfloat16)
     dense = lax.dot_general(place, tiles_ref[...], (((0,), (0,)), ((), ())), preferred_element_type=f32)
     out_ref[...] = dense.astype(jnp.bfloat16)
-    place_ref[...] = lax.rem(user_row, n_user) * (user_row.shape[1] // n_user) + lax.div(user_row, n_user)
-    same_ref[...] = weights_ref[...]
-
-
-def column_of(row, user_row, block_ids, tiles, weights, count, n_user):
+
+
+def column_of(row, user_row, block_ids, tiles, count):
     in_vmem = pl.BlockSpec(memory_space=pltpu.VMEM)
     return pl.pallas_call(
-        functools.partial(column_kernel, n_user),
-        out_shape=[
-            jax.ShapeDtypeStruct((count, tiles.shape[1]), jnp.bfloat16),
-            jax.ShapeDtypeStruct((1, user_row.shape[0]), jnp.int32),
-            jax.ShapeDtypeStruct((1, weights.shape[0]), f32),
-        ],
-        in_specs=[pl.BlockSpec(memory_space=pltpu.SMEM)] + [in_vmem] * 4,
-    )(row.reshape(1), user_row.reshape(1, -1), block_ids.T, tiles, weights.reshape(1, -1))
+        column_kernel,
+        out_shape=jax.ShapeDtypeStruct((count, tiles.shape[1]), jnp.bfloat16),
+        in_specs=[pl.BlockSpec(memory_space=pltpu.SMEM)] + [in_vmem] * 3,
+    )(row.reshape(1), user_row.reshape(1, -1), block_ids.T, tiles)
 
 
 def strips(at_ref, refs, flat_ref, users_ref):
@@ -299,24 +308,46 @@
     )(at, basis, *pieces)
 
 
-def wide_kernel(at_ref, basis_ref, x0_ref, x1_ref, x2_ref, x3_ref, out_ref, flat_ref, users_ref):
+def wide_kernel(
+    at_ref, basis_ref, x0_ref, x1_ref, x2_ref, x3_ref, user_row_ref, weights_ref,
+    out_ref, place_ref, same_ref, flat_ref, users_ref, row_ref, sems,
+):
+    fetch = pltpu.make_async_copy(user_row_ref, row_ref, sems.at[0])
+    hand_on = pltpu.make_async_copy(weights_ref, same_ref, sems.at[1])
+    fetch.start()
+    hand_on.start()
     parts = split(basis_ref[...])
     x = strips(at_ref, (x0_ref, x1_ref, x2_ref, x3_ref), flat_ref, users_ref)
     out_ref[:, :RANK] = parts[0]
     out_ref[:, RANK:ORDER] = jnp.transpose(x.astype(f32)).astype(jnp.bfloat16)
     out_ref[:, ORDER : ORDER + RANK] = parts[1]
     out_ref[:, ORDER + RANK :] = parts[2]
-
-
-def wide_of(at, basis, pieces):
-    in_vmem = pl.BlockSpec(memory_space=pltpu.VMEM)
+    fetch.wait()
+    hand_on.wait()
+    user_row = row_ref[...]
+    place_ref[...] = lax.rem(user_row, 4) * (user_row.shape[1] // 4) + lax.div(user_row, 4)
+
+
+def wide_of(at, basis, pieces, user_row, weights):
+    in_vmem, in_hbm = pl.BlockSpec(memory_space=pltpu.VMEM), pl.BlockSpec(memory_space=pltpu.HBM)
+    users = user_row.shape[0]
     return pl.pallas_call(
         wide_kernel,
-        out_shape=jax.ShapeDtypeStruct((basis.shape[0], ORDER + 2 * RANK), jnp.bfloat16),
-        in_specs=[pl.BlockSpec(memory_space=pltpu.SMEM)] + [in_vmem] * 5,
-        scratch_shapes=[pltpu.VMEM(pieces[0].shape, f32), pltpu.VMEM((USERS, basis.shape[0]), jnp.bfloat16)],
+        out_shape=[
+            jax.ShapeDtypeStruct((basis.shape[0], ORDER + 2 * RANK), jnp.bfloat16),
+            jax.ShapeDtypeStruct((1, users), jnp.int32),
+            jax.ShapeDtypeStruct((1, RANK), f32),
+        ],
+        in_specs=[pl.BlockSpec(memory_space=pltpu.SMEM)] + [in_vmem] * 5 + [in_hbm] * 2,
+        out_specs=[in_vmem] * 3,
+        scratch_shapes=[
+            pltpu.VMEM(pieces[0].shape, f32),
+            pltpu.VMEM((users, basis.shape[0]), jnp.bfloat16),
+            pltpu.VMEM((1, users), jnp.int32),
+            pltpu.SemaphoreType.DMA((2,)),
+        ],
         compiler_params=pltpu.CompilerParams(vmem_limit_bytes=32 * 2**20),
-    )(at, basis, *pieces)
+    )(at, basis, *pieces, user_row.reshape(1, -1), weights.reshape(1, -1))
 
 
 def around(x, axis):
@@ -330,27 +361,27 @@
 
 
 def summed(parts):
-    near = ("item_1", "item_2")
-    own = jnp.sum(lax.all_to_all(parts, near, 0, 0, tiled=True), axis=0)
+    own = jnp.sum(lax.all_to_all(parts, ("item_2", "item_1"), 0, 0, tiled=True), axis=0)
     own = jnp.sum(copies(own, "item_0"), axis=0)
-    return copies(own, (*near, "user")).reshape(-1, RANK)
+    half = copies(own, ("item_1", "user")).reshape(-1, RANK)
+    return half, lax.ppermute(half, "item_2", [(0, 1), (1, 0)])
 
 
 def per_device(basis, old_values, ratings, block_ids, user_row):
     n_item = lax.axis_size(ITEM)
-    n_user = lax.axis_size("user")
     width = ratings.shape[2]
     slab_blocks = basis.shape[0] // width
     user = lax.axis_index("user")
-    row = lax.axis_index(ITEM) * n_user + user
-    at = user.reshape(1)
-    column, place, weights = column_of(row, user_row, block_ids, ratings[0], old_values, n_item * slab_blocks, n_user)
+    row = lax.axis_index(ITEM) * lax.axis_size("user") + user
+    at = jnp.stack([user, lax.axis_index("item_2")]).astype(jnp.int32)
+    column = column_of(row, user_row, block_ids, ratings[0], n_item * slab_blocks)
     arrived = lax.all_to_all(column.reshape(n_item, slab_blocks, width), ITEM, 0, 0, tiled=True)
     arrived = arrived.reshape(n_item * slab_blocks, width)
     pieces = [arrived] + around(arrived, "user")
     parts = gram_parts(at, basis, pieces, lax.axis_size("item_1") * lax.axis_size("item_2"))
-    wide = wide_of(at, basis, pieces)
-    return tuple(core(summed(parts), wide, weights, place, basis.shape[0] * n_item))
+    wide, place, weights = wide_of(at, basis, pieces, user_row, old_values)
+    near, far = summed(parts)
+    return tuple(core(at, near, far, wide, weights, place, basis.shape[0] * n_item))
 
 
 def solution(mesh):

time: 91.6 us -> 86.5 us (0.944)
  blocking collectives: 41.4 us -> 51.2 us
  waiting for transfers between devices: 14.8 us -> 5.33 us
  starting transfers between devices: 9.6 us -> 6.99 us
  local copies, waits for them, and re-layouts: 1.49 us -> 0.03 us
  Pallas kernels: 23.2 us -> 21.9 us
    all_to_all x1 -> x2, blocking collectives: 9.83 us -> 19.6 us  [copies(): return lax.all_to_all(x, axes, split_axis=0, concat_axis=0, tiled=True)]
    all_to_all x1 -> x0, waiting for transfers between devices: 9.63 us -> none  [copies(): return lax.all_to_all(x, axes, split_axis=0, concat_axis=0, tiled=True)]
    all_to_all x1 -> x0, starting transfers between devices: 5.83 us -> none  [copies(): return lax.all_to_all(x, axes, split_axis=0, concat_axis=0, tiled=True)]
    ppermute x0 -> x1, starting transfers between devices: none -> 3.22 us  [summed(): return (half, lax.ppermute(half, 'item_2', [(0, 1), (1, 0)]))]
    pallas_call x1, Pallas kernels: 20.5 us -> 18.1 us  [core(): pl.pallas_call(functools.partial(core_kernel, items), out_shape=[jax.Shap...]
  transfers between devices with their start and end apart: 4 -> 4, of which waited for: 4 -> 4; matrix products, arithmetic and copies ran while one was open for 0% -> 0% of each run, Pallas kernels for 0% -> 1%
where the time goes in v4:
time: 86.5 us; the launch traced here: 86.2 us
  blocking collectives  51.2 us (59%)
  Pallas kernels  21.9 us (25%)
  starting transfers between devices  6.99 us (8%)
  waiting for transfers between devices  5.33 us (6%)
    all_to_all x1, blocking collectives, per_device(): lax.all_to_all(column.reshape(n_item, slab_blocks, width), ITEM, 0, 0, ti...  23.1 us
    all_to_all x2, blocking collectives, copies(): return lax.all_to_all(x, axes, split_axis=0, concat_axis=0, tiled=True)  19.6 us
    pallas_call x1, Pallas kernels, core(): pl.pallas_call(functools.partial(core_kernel, items), out_shape=[jax.Shap...  18.1 us
    all_to_all x1, blocking collectives, summed(): lax.all_to_all(parts, ('item_2', 'item_1'), 0, 0, tiled=True)  8.55 us
    ppermute x3, waiting for transfers between devices, around(): lax.ppermute(x, axis, [(i, (i + k) % n) for i in range(n)])  5.14 us
    ppermute x3, starting transfers between devices, around(): lax.ppermute(x, axis, [(i, (i + k) % n) for i in range(n)])  3.77 us
    ppermute x1, starting transfers between devices, summed(): return (half, lax.ppermute(half, 'item_2', [(0, 1), (1, 0)]))  3.22 us
    pallas_call x1, Pallas kernels, column_of(): pl.pallas_call(column_kernel, out_shape=jax.ShapeDtypeStruct((count, tile...  1.8 us
  transfers between devices with their start and end apart: 4, of which 4 were waited for; matrix products, arithmetic and copies ran while one was open for 0% of the time, Pallas kernels for 1%

profile of v4, /device:TPU:1, one launch (start us, length us, event | category | flops | bytes accessed | tf_op | source)
XLA Modules:
  0.0 86.2 jit_solution(16542633888258817873)
XLA Ops:
  0.6 0.0 copy-start
  0.7 1.8 %shard_map.68 = bf16[256,128]{1,0:T(8,128)(2,1)} custom-call(s32[1]{0:T(128)} %bitcast.2.row_ref, s32[1,256]{1,0:T(1,128)} %bitcast.17, s32[64,256]{1,0:T(8,128)} %bitcast.21, bf16[64,128]{1,0:T(8,128)(2,1)} %bitcast.22), custom_call_target="tpu_custom_call" | custom-call | tf_op jit(solution)/shard_map/pallas_call | solution.py:256
  2.5 23.1 %all_to_all.20 = bf16[64,4,128]{2,1,0:T(4,128)(2,1)S(1)} all-to-all(bf16[64,4,128]{2,1,0:T(4,128)(2,1)} %bitcast.20), channel_id=1, replica_groups=mesh['item_0'=8,'item_1'=4,'item_2'=2,'user'=4] {'item_0','item_1','item..., dimensions={0} | all-to-all | bytes 131072 | tf_op jit(solution)/shard_map/all_to_all | solution.py:378
  25.5 2.7 %collective-permute-start.2 = (bf16[256,128]{1,0:T(8,128)(2,1)S(1)}, bf16[256,128]{1,0:T(8,128)(2,1)S(1)}, u32[]{:S(2)}, u32[]{:S(2)}) collective-permute-start(bf16[256,128]{1,0:T(8,128)(2,1)S(1)} %bitcast.12), channel_id=1, source_target_pairs={{0,3},{1,0},{2,1},{3,2},{4,7},{5,4},{6,5},{7,6},{8,11},{9,8},{10,9... | collective-permute-start | bytes 196616 | tf_op jit(solution)/shard_map/ppermute | solution.py:355
  28.3 0.3 collective-permute-start.1
  28.6 0.7 collective-permute-start
  29.3 0.1 pad_add_fusion.at_ref
  29.4 0.2 collective-permute-done.2.x3_ref
  29.6 3.4 %collective-permute-done.1.x2_ref = bf16[256,128]{1,0:T(8,128)(2,1)S(1)} collective-permute-done((bf16[256,128]{1,0:T(8,128)(2,1)S(1)}, bf16[256,128]{1,0:T(8,128)(2,1)S(1)}, u32[]{:S(2)}, u32[]{:S(2)}) %collective-permute-start.1) | collective-permute-done | bytes 65568 | tf_op jit(solution)/shard_map/ppermute | solution.py:355
  32.9 1.6 %collective-permute-done.x1_ref = bf16[256,128]{1,0:T(8,128)(2,1)S(1)} collective-permute-done((bf16[256,128]{1,0:T(8,128)(2,1)S(1)}, bf16[256,128]{1,0:T(8,128)(2,1)S(1)}, u32[]{:S(2)}, u32[]{:S(2)}) %collective-permute-start) | collective-permute-done | bytes 65568 | tf_op jit(solution)/shard_map/ppermute | solution.py:355
  34.5 0.0 copy-done
  34.5 1.1 %shard_map.69 = f32[8,24,128]{2,1,0:T(8,128)S(1)} custom-call(s32[2]{0:T(128)S(1)} %pad_add_fusion.at_ref, f32[512,128]{1,0:T(8,128)S(1)} %copy-done, bf16[256,128]{1,0:T(8,128)(2,1)S(1)} %bitcast.15, bf16[256,128]{1,0:T(8,128)(2,1)S(1)} %collective-permute-done.x1_ref, bf16[256,128]{1,0:T(8,128)(2,1)S(1)} %collective-permute-done.1.x2_ref, ...), custom_call_target="tpu_custom_call" | custom-call | tf_op jit(solution)/shard_map/pallas_call | solution.py:298
  35.7 8.5 %all_to_all.21 = f32[8,24,128]{2,1,0:T(8,128)S(1)} all-to-all(f32[8,24,128]{2,1,0:T(8,128)S(1)} %shard_map.69), channel_id=1, replica_groups=mesh['item_0'=8,'item_1'=4,'item_2'=2,'user'=4] {'item_2','item_1'}, dimensions={0} | all-to-all | bytes 196608 | tf_op jit(solution)/shard_map/all_to_all | solution.py:364
  44.2 9.9 %all_to_all.22 = f32[8,24,128]{2,1,0:T(8,128)S(1)} all-to-all(f32[8,24,128]{2,1,0:T(8,128)S(1)} %broadcast_in_dim.6), channel_id=1, replica_groups=mesh['item_0'=8,'item_1'=4,'item_2'=2,'user'=4] {'item_0'}, dimensions={0} | all-to-all | bytes 196608 | tf_op jit(solution)/shard_map/all_to_all | solution.py:360
  54.2 9.7 %all_to_all.23 = f32[16,24,128]{2,1,0:T(8,128)S(1)} all-to-all(f32[16,24,128]{2,1,0:T(8,128)S(1)} %broadcast_in_dim.7), channel_id=1, replica_groups=mesh['item_0'=8,'item_1'=4,'item_2'=2,'user'=4] {'item_1','user'}, dimensions={0} | all-to-all | bytes 393216 | tf_op jit(solution)/shard_map/all_to_all | solution.py:360
  63.9 0.0 copy-start.1
  63.9 0.0 copy-start.2
  63.9 3.2 %collective-permute-start.3 = (f32[384,128]{1,0:T(8,128)S(1)}, f32[384,128]{1,0:T(8,128)S(1)}, u32[]{:S(2)}, u32[]{:S(2)}) collective-permute-start(f32[384,128]{1,0:T(8,128)S(1)} %bitcast.10), channel_id=1, source_target_pairs={{0,4},{4,0},{1,5},{5,1},{2,6},{6,2},{3,7},{7,3},{8,12},{12,8},{9,1... | collective-permute-start | bytes 589832 | tf_op jit(solution)/shard_map/ppermute | solution.py:367
  67.1 0.0 copy-done.1
  67.1 0.0 copy-done.2
  67.1 0.9 %shard_map.70 = (bf16[512,640]{1,0:T(8,128)(2,1)S(1)}, s32[1,256]{1,0:T(1,128)S(1)}, f32[1,128]{1,0:T(1,128)S(1)}) custom-call(s32[2]{0:T(128)S(1)} %pad_add_fusion.at_ref, f32[512,128]{1,0:T(8,128)S(1)} %copy-done, bf16[256,128]{1,0:T(8,128)(2,1)S(1)} %bitcast.16, bf16[256,128]{1,0:T(8,128)(2,1)S(1)} %collective-permute-done.x1_ref, ...), custom_call_target="tpu_custom_call" | custom-call | tf_op jit(solution)/shard_map/pallas_call | solution.py:334
  68.0 0.2 collective-permute-done.3.far_ref
  68.2 18.1 %shard_map.71 = (f32[512,128]{1,0:T(8,128)}, f32[256,128]{1,0:T(8,128)}) custom-call(s32[2]{0:T(128)S(1)} %pad_add_fusion.at_ref, f32[384,128]{1,0:T(8,128)S(1)} %bitcast.11, f32[384,128]{1,0:T(8,128)S(1)} %collective-permute-done.3.far_ref, bf16[512,640]{1,0:T(8,128)(2,1)S(1)} %get-tuple-element.5.wide_ref, f32[1,128]{1,0:T(1,128)S(1)} %get-tuple-element.6.weights_ref, ...), custom_call_target="tpu_custom_call" | custom-call | tf_op jit(solution)/shard_map/pallas_call | solution.py:230
  (4 shorter events, 0.0 us)
Async XLA Ops:
  0.6 33.9 %copy-start = (f32[512,128]{1,0:T(8,128)S(1)}, f32[512,128]{1,0:T(8,128)}, u32[]{:S(2)}) copy-start(f32[512,128]{1,0:T(8,128)} %basis_ref.3) | copy-start | bytes 786436
  25.5 4.1 %collective-permute-start.2 = (bf16[256,128]{1,0:T(8,128)(2,1)S(1)}, bf16[256,128]{1,0:T(8,128)(2,1)S(1)}, u32[]{:S(2)}, u32[]{:S(2)}) collective-permute-start(bf16[256,128]{1,0:T(8,128)(2,1)S(1)} %bitcast.12), channel_id=1, source_target_pairs={{0,3},{1,0},{2,1},{3,2},{4,7},{5,4},{6,5},{7,6},{8,11},{9,8},{10,9... | collective-permute-start | bytes 196616 | tf_op jit(solution)/shard_map/ppermute | solution.py:355
  28.3 4.7 %collective-permute-start.1 = (bf16[256,128]{1,0:T(8,128)(2,1)S(1)}, bf16[256,128]{1,0:T(8,128)(2,1)S(1)}, u32[]{:S(2)}, u32[]{:S(2)}) collective-permute-start(bf16[256,128]{1,0:T(8,128)(2,1)S(1)} %bitcast.13), channel_id=1, source_target_pairs={{0,2},{1,3},{2,0},{3,1},{4,6},{5,7},{6,4},{7,5},{8,10},{9,11},{10,... | collective-permute-start | bytes 196616 | tf_op jit(solution)/shard_map/ppermute | solution.py:355
  28.6 5.9 %collective-permute-start = (bf16[256,128]{1,0:T(8,128)(2,1)S(1)}, bf16[256,128]{1,0:T(8,128)(2,1)S(1)}, u32[]{:S(2)}, u32[]{:S(2)}) collective-permute-start(bf16[256,128]{1,0:T(8,128)(2,1)S(1)} %bitcast.14), channel_id=1, source_target_pairs={{0,1},{1,2},{2,3},{3,0},{4,5},{5,6},{6,7},{7,4},{8,9},{9,10},{10,1... | collective-permute-start | bytes 196616 | tf_op jit(solution)/shard_map/ppermute | solution.py:355
  63.9 3.2 %copy-start.1 = (s32[256]{0:T(256)S(1)}, s32[256]{0:T(256)}, u32[]{:S(2)}) copy-start(s32[256]{0:T(256)} %param.9) | copy-start | bytes 3076
  63.9 3.2 %copy-start.2 = (f32[128]{0:T(128)S(1)}, f32[128]{0:T(128)}, u32[]{:S(2)}) copy-start(f32[128]{0:T(128)} %param.6) | copy-start | bytes 1540
  63.9 4.3 %collective-permute-start.3 = (f32[384,128]{1,0:T(8,128)S(1)}, f32[384,128]{1,0:T(8,128)S(1)}, u32[]{:S(2)}, u32[]{:S(2)}) collective-permute-start(f32[384,128]{1,0:T(8,128)S(1)} %bitcast.10), channel_id=1, source_target_pairs={{0,4},{4,0},{1,5},{5,1},{2,6},{6,2},{3,7},{7,3},{8,12},{12,8},{9,1... | collective-permute-start | bytes 589832 | tf_op jit(solution)/shard_map/ppermute | solution.py:367

commit v5 on v4

--- a/solution.py
+++ b/solution.py
@@ -161,11 +161,11 @@
 
 
 def core_kernel(
-    items, at_ref, near_ref, far_ref, wide_ref, weights_ref, place_ref,
+    items, core_ref, near_ref, far_ref, wide_ref, weights_ref, place_ref,
     rows_ref, factors_ref, sums_ref, gram_ref, turn_t_ref, back_ref,
 ):
     half = near_ref.shape[0]
-    for place, ref in ((at_ref[1], near_ref), (1 - at_ref[1], far_ref)):
+    for place, ref in ((core_ref[0], near_ref), (1 - core_ref[0], far_ref)):
         sums_ref[pl.ds(pl.multiple_of(place * half, 8), half), :] = ref[...]
     weights = weights_ref[...]
     whole, size = assemble(sums_ref, weights, items)
@@ -225,7 +225,7 @@
     factors_ref[...] = jnp.transpose(found)
 
 
-def core(at, near, far, wide, weights, place, items):
+def core(here, near, far, wide, weights, place, items):
     in_vmem = pl.BlockSpec(memory_space=pltpu.VMEM)
     return pl.pallas_call(
         functools.partial(core_kernel, items),
@@ -238,7 +238,7 @@
             pltpu.VMEM((RANK, ORDER), f32),
         ],
         compiler_params=pltpu.CompilerParams(vmem_limit_bytes=32 * 2**20),
-    )(at, near, far, wide, weights, place)
+    )(here, near, far, wide, weights, place)
 
 
 def column_kernel(row_ref, user_row_ref, blocks_ref, tiles_ref, out_ref):
@@ -260,20 +260,20 @@
     )(row.reshape(1), user_row.reshape(1, -1), block_ids.T, tiles)
 
 
-def strips(at_ref, refs, flat_ref, users_ref):
-    count = flat_ref.shape[0] // CAP
+def strips(user_ref, refs, fluser_ref, users_ref):
+    count = fluser_ref.shape[0] // CAP
     owners = len(refs)
     for k, ref in enumerate(refs):
-        flat_ref[...] = ref[...].astype(f32)
-        blocks = [flat_ref[pl.ds(b, count, stride=CAP), :] for b in range(CAP)]
-        owner = lax.rem(at_ref[0] + owners - k, owners)
+        fluser_ref[...] = ref[...].astype(f32)
+        blocks = [fluser_ref[pl.ds(b, count, stride=CAP), :] for b in range(CAP)]
+        owner = lax.rem(user_ref[0] + owners - k, owners)
         here = pl.ds(pl.multiple_of(owner * count, 16), count)
         users_ref[here, :] = jnp.concatenate(blocks, axis=1).astype(jnp.bfloat16)
     return users_ref[...]
 
 
-def gram_kernel(at_ref, basis_ref, x0_ref, x1_ref, x2_ref, x3_ref, out_ref, flat_ref, users_ref, all_ref):
-    x = strips(at_ref, (x0_ref, x1_ref, x2_ref, x3_ref), flat_ref, users_ref)
+def gram_kernel(user_ref, basis_ref, x0_ref, x1_ref, x2_ref, x3_ref, out_ref, fluser_ref, users_ref, all_ref):
+    x = strips(user_ref, (x0_ref, x1_ref, x2_ref, x3_ref), fluser_ref, users_ref)
     parts = split(basis_ref[...])
     high_t, middle_t = (jnp.transpose(p.astype(f32)).astype(jnp.bfloat16) for p in parts[:2])
     one = lambda a, b: jnp.dot(a, b, preferred_element_type=f32)
@@ -289,11 +289,11 @@
     all_ref[5 * RANK :, :] = cross[RANK:, RANK:]
     count, piece = out_ref.shape[:2]
     for k in range(count):
-        first = (k * 4 + at_ref[0]) * piece
+        first = (k * 4 + user_ref[0]) * piece
         out_ref[k] = all_ref[pl.ds(pl.multiple_of(first, 8), piece), :]
 
 
-def gram_parts(at, basis, pieces, count):
+def gram_parts(user, basis, pieces, count):
     in_vmem = pl.BlockSpec(memory_space=pltpu.VMEM)
     return pl.pallas_call(
         gram_kernel,
@@ -305,19 +305,19 @@
             pltpu.VMEM((6 * RANK, RANK), f32),
         ],
         compiler_params=pltpu.CompilerParams(vmem_limit_bytes=32 * 2**20),
-    )(at, basis, *pieces)
+    )(user, basis, *pieces)
 
 
 def wide_kernel(
-    at_ref, basis_ref, x0_ref, x1_ref, x2_ref, x3_ref, user_row_ref, weights_ref,
-    out_ref, place_ref, same_ref, flat_ref, users_ref, row_ref, sems,
+    user_ref, basis_ref, x0_ref, x1_ref, x2_ref, x3_ref, user_row_ref, weights_ref,
+    out_ref, place_ref, same_ref, fluser_ref, users_ref, row_ref, sems,
 ):
     fetch = pltpu.make_async_copy(user_row_ref, row_ref, sems.at[0])
     hand_on = pltpu.make_async_copy(weights_ref, same_ref, sems.at[1])
     fetch.start()
     hand_on.start()
     parts = split(basis_ref[...])
-    x = strips(at_ref, (x0_ref, x1_ref, x2_ref, x3_ref), flat_ref, users_ref)
+    x = strips(user_ref, (x0_ref, x1_ref, x2_ref, x3_ref), fluser_ref, users_ref)
     out_ref[:, :RANK] = parts[0]
     out_ref[:, RANK:ORDER] = jnp.transpose(x.astype(f32)).astype(jnp.bfloat16)
     out_ref[:, ORDER : ORDER + RANK] = parts[1]
@@ -328,7 +328,7 @@
     place_ref[...] = lax.rem(user_row, 4) * (user_row.shape[1] // 4) + lax.div(user_row, 4)
 
 
-def wide_of(at, basis, pieces, user_row, weights):
+def wide_of(user, basis, pieces, user_row, weights):
     in_vmem, in_hbm = pl.BlockSpec(memory_space=pltpu.VMEM), pl.BlockSpec(memory_space=pltpu.HBM)
     users = user_row.shape[0]
     return pl.pallas_call(
@@ -347,7 +347,7 @@
             pltpu.SemaphoreType.DMA((2,)),
         ],
         compiler_params=pltpu.CompilerParams(vmem_limit_bytes=32 * 2**20),
-    )(at, basis, *pieces, user_row.reshape(1, -1), weights.reshape(1, -1))
+    )(user, basis, *pieces, user_row.reshape(1, -1), weights.reshape(1, -1))
 
 
 def around(x, axis):
@@ -371,17 +371,16 @@
     n_item = lax.axis_size(ITEM)
     width = ratings.shape[2]
     slab_blocks = basis.shape[0] // width
-    user = lax.axis_index("user")
-    row = lax.axis_index(ITEM) * lax.axis_size("user") + user
-    at = jnp.stack([user, lax.axis_index("item_2")]).astype(jnp.int32)
+    user, here = lax.axis_index("user").reshape(1), lax.axis_index("item_2").reshape(1)
+    row = lax.axis_index(ITEM) * lax.axis_size("user") + lax.axis_index("user")
     column = column_of(row, user_row, block_ids, ratings[0], n_item * slab_blocks)
     arrived = lax.all_to_all(column.reshape(n_item, slab_blocks, width), ITEM, 0, 0, tiled=True)
     arrived = arrived.reshape(n_item * slab_blocks, width)
     pieces = [arrived] + around(arrived, "user")
-    parts = gram_parts(at, basis, pieces, lax.axis_size("item_1") * lax.axis_size("item_2"))
-    wide, place, weights = wide_of(at, basis, pieces, user_row, old_values)
+    parts = gram_parts(user, basis, pieces, lax.axis_size("item_1") * lax.axis_size("item_2"))
+    wide, place, weights = wide_of(user, basis, pieces, user_row, old_values)
     near, far = summed(parts)
-    return tuple(core(at, near, far, wide, weights, place, basis.shape[0] * n_item))
+    return tuple(core(here, near, far, wide, weights, place, basis.shape[0] * n_item))
 
 
 def solution(mesh):

time: 86.5 us -> 85.5 us (0.988)
  Pallas kernels: 21.9 us -> 20.3 us
  transfers between devices with their start and end apart: 4 -> 4, of which waited for: 4 -> 4; matrix products, arithmetic and copies ran while one was open for 0% -> 0% of each run, Pallas kernels for 1% -> 0%
where the time goes in v5:
time: 85.5 us; the launch traced here: 85.1 us
  blocking collectives  51.2 us (60%)
  Pallas kernels  20.3 us (24%)
  starting transfers between devices  6.99 us (8%)
  waiting for transfers between devices  5.94 us (7%)
    all_to_all x1, blocking collectives, per_device(): lax.all_to_all(column.reshape(n_item, slab_blocks, width), ITEM, 0, 0, ti...  23.1 us
    all_to_all x2, blocking collectives, copies(): return lax.all_to_all(x, axes, split_axis=0, concat_axis=0, tiled=True)  19.6 us
    pallas_call x1, Pallas kernels, core(): pl.pallas_call(functools.partial(core_kernel, items), out_shape=[jax.Shap...  17.5 us
    all_to_all x1, blocking collectives, summed(): lax.all_to_all(parts, ('item_2', 'item_1'), 0, 0, tiled=True)  8.55 us
    ppermute x3, waiting for transfers between devices, around(): lax.ppermute(x, axis, [(i, (i + k) % n) for i in range(n)])  5.21 us
    ppermute x3, starting transfers between devices, around(): lax.ppermute(x, axis, [(i, (i + k) % n) for i in range(n)])  3.77 us
    ppermute x1, starting transfers between devices, summed(): return (half, lax.ppermute(half, 'item_2', [(0, 1), (1, 0)]))  3.21 us
    pallas_call x1, Pallas kernels, column_of(): pl.pallas_call(column_kernel, out_shape=jax.ShapeDtypeStruct((count, tile...  1.8 us
  transfers between devices with their start and end apart: 4, of which 4 were waited for; matrix products, arithmetic and copies ran while one was open for 0% of the time, Pallas kernels for 0%

profile of v5, /device:TPU:1, one launch (start us, length us, event | category | flops | bytes accessed | tf_op | source)
XLA Modules:
  0.0 85.1 jit_solution(2344002488251381532)
XLA Ops:
  0.6 0.0 copy-start
  0.7 1.8 %shard_map.68 = bf16[256,128]{1,0:T(8,128)(2,1)} custom-call(s32[1]{0:T(128)} %bitcast.2.row_ref, s32[1,256]{1,0:T(1,128)} %bitcast.17, s32[64,256]{1,0:T(8,128)} %bitcast.21, bf16[64,128]{1,0:T(8,128)(2,1)} %bitcast.22), custom_call_target="tpu_custom_call" | custom-call | tf_op jit(solution)/shard_map/pallas_call | solution.py:256
  2.5 23.1 %all_to_all.20 = bf16[64,4,128]{2,1,0:T(4,128)(2,1)S(1)} all-to-all(bf16[64,4,128]{2,1,0:T(4,128)(2,1)} %bitcast.20), channel_id=1, replica_groups=mesh['item_0'=8,'item_1'=4,'item_2'=2,'user'=4] {'item_0','item_1','item..., dimensions={0} | all-to-all | bytes 131072 | tf_op jit(solution)/shard_map/all_to_all | solution.py:377
  25.5 2.7 %collective-permute-start.2 = (bf16[256,128]{1,0:T(8,128)(2,1)S(1)}, bf16[256,128]{1,0:T(8,128)(2,1)S(1)}, u32[]{:S(2)}, u32[]{:S(2)}) collective-permute-start(bf16[256,128]{1,0:T(8,128)(2,1)S(1)} %bitcast.12), channel_id=1, source_target_pairs={{0,3},{1,0},{2,1},{3,2},{4,7},{5,4},{6,5},{7,6},{8,11},{9,8},{10,9... | collective-permute-start | bytes 196616 | tf_op jit(solution)/shard_map/ppermute | solution.py:355
  28.3 0.3 collective-permute-start.1
  28.6 0.7 collective-permute-start
  29.3 0.3 collective-permute-done.2.x3_ref
  29.6 3.4 %collective-permute-done.1.x2_ref = bf16[256,128]{1,0:T(8,128)(2,1)S(1)} collective-permute-done((bf16[256,128]{1,0:T(8,128)(2,1)S(1)}, bf16[256,128]{1,0:T(8,128)(2,1)S(1)}, u32[]{:S(2)}, u32[]{:S(2)}) %collective-permute-start.1) | collective-permute-done | bytes 65568 | tf_op jit(solution)/shard_map/ppermute | solution.py:355
  32.9 1.6 %collective-permute-done.x1_ref = bf16[256,128]{1,0:T(8,128)(2,1)S(1)} collective-permute-done((bf16[256,128]{1,0:T(8,128)(2,1)S(1)}, bf16[256,128]{1,0:T(8,128)(2,1)S(1)}, u32[]{:S(2)}, u32[]{:S(2)}) %collective-permute-start) | collective-permute-done | bytes 65568 | tf_op jit(solution)/shard_map/ppermute | solution.py:355
  34.5 0.0 copy-done
  34.5 0.6 shard_map.69
  35.1 8.5 %all_to_all.21 = f32[8,24,128]{2,1,0:T(8,128)S(1)} all-to-all(f32[8,24,128]{2,1,0:T(8,128)S(1)} %shard_map.69), channel_id=1, replica_groups=mesh['item_0'=8,'item_1'=4,'item_2'=2,'user'=4] {'item_2','item_1'}, dimensions={0} | all-to-all | bytes 196608 | tf_op jit(solution)/shard_map/all_to_all | solution.py:364
  43.7 9.9 %all_to_all.22 = f32[8,24,128]{2,1,0:T(8,128)S(1)} all-to-all(f32[8,24,128]{2,1,0:T(8,128)S(1)} %broadcast_in_dim.6), channel_id=1, replica_groups=mesh['item_0'=8,'item_1'=4,'item_2'=2,'user'=4] {'item_0'}, dimensions={0} | all-to-all | bytes 196608 | tf_op jit(solution)/shard_map/all_to_all | solution.py:360
  53.7 9.7 %all_to_all.23 = f32[16,24,128]{2,1,0:T(8,128)S(1)} all-to-all(f32[16,24,128]{2,1,0:T(8,128)S(1)} %broadcast_in_dim.7), channel_id=1, replica_groups=mesh['item_0'=8,'item_1'=4,'item_2'=2,'user'=4] {'item_1','user'}, dimensions={0} | all-to-all | bytes 393216 | tf_op jit(solution)/shard_map/all_to_all | solution.py:360
  63.3 0.0 copy-start.1
  63.3 0.0 copy-start.2
  63.3 3.2 %collective-permute-start.3 = (f32[384,128]{1,0:T(8,128)S(1)}, f32[384,128]{1,0:T(8,128)S(1)}, u32[]{:S(2)}, u32[]{:S(2)}) collective-permute-start(f32[384,128]{1,0:T(8,128)S(1)} %bitcast.10), channel_id=1, source_target_pairs={{0,4},{4,0},{1,5},{5,1},{2,6},{6,2},{3,7},{7,3},{8,12},{12,8},{9,1... | collective-permute-start | bytes 589832 | tf_op jit(solution)/shard_map/ppermute | solution.py:367
  66.6 0.0 copy-done.1
  66.6 0.0 copy-done.2
  66.6 0.3 shard_map.70
  66.9 0.7 collective-permute-done.3.far_ref
  67.6 17.5 %shard_map.71 = (f32[512,128]{1,0:T(8,128)}, f32[256,128]{1,0:T(8,128)}) custom-call(s32[1]{0:T(128)} %bitcast.core_ref, f32[384,128]{1,0:T(8,128)S(1)} %bitcast.11, f32[384,128]{1,0:T(8,128)S(1)} %collective-permute-done.3.far_ref, bf16[512,640]{1,0:T(8,128)(2,1)S(1)} %get-tuple-element.5.wide_ref, f32[1,128]{1,0:T(1,128)S(1)} %get-tuple-element.6.weights_ref, ...), custom_call_target="tpu_custom_call" | custom-call | tf_op jit(solution)/shard_map/pallas_call | solution.py:230
  (4 shorter events, 0.0 us)
Async XLA Ops:
  0.6 33.9 %copy-start = (f32[512,128]{1,0:T(8,128)S(1)}, f32[512,128]{1,0:T(8,128)}, u32[]{:S(2)}) copy-start(f32[512,128]{1,0:T(8,128)} %basis_ref.3) | copy-start | bytes 786436
  25.5 4.1 %collective-permute-start.2 = (bf16[256,128]{1,0:T(8,128)(2,1)S(1)}, bf16[256,128]{1,0:T(8,128)(2,1)S(1)}, u32[]{:S(2)}, u32[]{:S(2)}) collective-permute-start(bf16[256,128]{1,0:T(8,128)(2,1)S(1)} %bitcast.12), channel_id=1, source_target_pairs={{0,3},{1,0},{2,1},{3,2},{4,7},{5,4},{6,5},{7,6},{8,11},{9,8},{10,9... | collective-permute-start | bytes 196616 | tf_op jit(solution)/shard_map/ppermute | solution.py:355
  28.3 4.7 %collective-permute-start.1 = (bf16[256,128]{1,0:T(8,128)(2,1)S(1)}, bf16[256,128]{1,0:T(8,128)(2,1)S(1)}, u32[]{:S(2)}, u32[]{:S(2)}) collective-permute-start(bf16[256,128]{1,0:T(8,128)(2,1)S(1)} %bitcast.13), channel_id=1, source_target_pairs={{0,2},{1,3},{2,0},{3,1},{4,6},{5,7},{6,4},{7,5},{8,10},{9,11},{10,... | collective-permute-start | bytes 196616 | tf_op jit(solution)/shard_map/ppermute | solution.py:355
  28.6 5.9 %collective-permute-start = (bf16[256,128]{1,0:T(8,128)(2,1)S(1)}, bf16[256,128]{1,0:T(8,128)(2,1)S(1)}, u32[]{:S(2)}, u32[]{:S(2)}) collective-permute-start(bf16[256,128]{1,0:T(8,128)(2,1)S(1)} %bitcast.14), channel_id=1, source_target_pairs={{0,1},{1,2},{2,3},{3,0},{4,5},{5,6},{6,7},{7,4},{8,9},{9,10},{10,1... | collective-permute-start | bytes 196616 | tf_op jit(solution)/shard_map/ppermute | solution.py:355
  63.3 3.2 %copy-start.1 = (s32[256]{0:T(256)S(1)}, s32[256]{0:T(256)}, u32[]{:S(2)}) copy-start(s32[256]{0:T(256)} %param.9) | copy-start | bytes 3076
  63.3 3.2 %copy-start.2 = (f32[128]{0:T(128)S(1)}, f32[128]{0:T(128)}, u32[]{:S(2)}) copy-start(f32[128]{0:T(128)} %param.6) | copy-start | bytes 1540
  63.3 4.3 %collective-permute-start.3 = (f32[384,128]{1,0:T(8,128)S(1)}, f32[384,128]{1,0:T(8,128)S(1)}, u32[]{:S(2)}, u32[]{:S(2)}) collective-permute-start(f32[384,128]{1,0:T(8,128)S(1)} %bitcast.10), channel_id=1, source_target_pairs={{0,4},{4,0},{1,5},{5,1},{2,6},{6,2},{3,7},{7,3},{8,12},{12,8},{9,1... | collective-permute-start | bytes 589832 | tf_op jit(solution)/shard_map/ppermute | solution.py:367

commit v6 on v5

--- a/solution.py
+++ b/solution.py
@@ -51,56 +51,59 @@
     lane = lax.broadcasted_iota(jnp.int32, (8, RANK), 1)
     sub = lax.broadcasted_iota(jnp.int32, (8, RANK), 0)
     count = RANK // 8
+    width = 16
+    deep = width // 8
     rows = [gram[8 * k : 8 * k + 8, :] for k in range(count)]
     pivots = []
-    for panel in range(count):
-        here = rows[panel]
+    for panel in range(0, count, deep):
         first = 8 * panel
-        column = [spread(here[:, first + k : first + k + 1]) for k in range(8)]
-        pivot_of_row = jnp.ones((8, RANK), f32)
+        column = [[spread(rows[panel + q][:, first + k : first + k + 1]) for k in range(width)] for q in range(deep)]
+        marks = [jnp.ones((8, RANK), f32) for _ in range(deep)]
         steps = []
-        for s in range(0, 8, 2):
-            upper = [spread(column[k][s : s + 1, :]) for k in range(s, 8)]
-            under = [spread(column[k][s + 1 : s + 2, :]) for k in range(s + 1, 8)]
+        for s in range(0, width, 2):
+            at, r = divmod(s, 8)
+            upper = [spread(column[at][k][r : r + 1, :]) for k in range(s, width)]
+            under = [spread(column[at][k][r + 1 : r + 2, :]) for k in range(s + 1, width)]
             a, b, c = upper[0], upper[1], under[0]
             det = a * c - b * b
             inverse = 1.0 / a
             second = 1.0 / det
             ratio = b * inverse
-            line = spread(here[s : s + 1, :])
+            line = spread(rows[panel + at][r : r + 1, :])
             line = jnp.where(lane == first + s, line + line, line)
-            next_line = spread(here[s + 1 : s + 2, :]) - ratio * line
+            next_line = spread(rows[panel + at][r + 1 : r + 2, :]) - ratio * line
             next_line = jnp.where(lane == first + s + 1, next_line + next_line, next_line)
-            pivot_of_row = jnp.where(sub == s, a, jnp.where(sub == s + 1, det * inverse, pivot_of_row))
+            marks[at] = jnp.where(sub == r, a, jnp.where(sub == r + 1, det * inverse, marks[at]))
             next_inverse, mixed = a * second, b * second
             under = [x - ratio * y for x, y in zip(under, upper[1:])]
             steps.append((inverse, line, upper))
             steps.append((next_inverse, next_line, under))
-            one = jnp.where(sub > s, column[s] * inverse, 0.0)
-            two = jnp.where(sub > s + 1, column[s + 1] * next_inverse - column[s] * mixed, 0.0)
-            here = here - one * line - two * next_line
-            for k in range(s + 2, 8):
-                column[k] = column[k] - one * upper[k - s] - two * under[k - s - 1]
-        rows[panel] = here
-        pivots.append(pivot_of_row)
-        for other in range(panel + 1, min(panel + 2, count)):
+            for q in range(at, deep):
+                one, two = column[q][s] * inverse, column[q][s + 1] * next_inverse - column[q][s] * mixed
+                if q == at:
+                    one, two = jnp.where(sub > r, one, 0.0), jnp.where(sub > r + 1, two, 0.0)
+                rows[panel + q] = rows[panel + q] - one * line - two * next_line
+                for k in range(s + 2, width):
+                    column[q][k] = column[q][k] - one * upper[k - s] - two * under[k - s - 1]
+        pivots += marks
+        for other in range(panel + deep, min(panel + deep + 2, count)):
             there = rows[other]
-            column = [spread(there[:, first + k : first + k + 1]) for k in range(8)]
+            column = [spread(there[:, first + k : first + k + 1]) for k in range(width)]
             for s, (inverse, line, upper) in enumerate(steps):
                 factor = column[s] * inverse
                 there = there - factor * line
-                for k in range(s + 1, 8):
+                for k in range(s + 1, width):
                     column[k] = column[k] - factor * upper[k - s]
             rows[other] = there
-        solved = [None] * 8
-        for s in range(7, -1, -1):
+        solved = [None] * width
+        for s in range(width - 1, -1, -1):
             inverse, line, upper = steps[s]
-            for k in range(s + 1, 8):
+            for k in range(s + 1, width):
                 line = line - upper[k - s] * solved[k]
             solved[s] = line * inverse
-        for other in range(panel + 2, count):
+        for other in range(panel + deep + 2, count):
             there = rows[other]
-            for k in range(8):
+            for k in range(width):
                 there = there - spread(rows[other][:, first + k : first + k + 1]) * solved[k]
             rows[other] = there
     return lower_of(jnp.concatenate(rows, axis=0)), jnp.concatenate(pivots, axis=0)
@@ -163,7 +166,19 @@
 def core_kernel(
     items, core_ref, near_ref, far_ref, wide_ref, weights_ref, place_ref,
     rows_ref, factors_ref, sums_ref, gram_ref, turn_t_ref, back_ref,
+    factored_ref, lower_ref, pivots_ref,
 ):
+    def apart(gram):
+        factored_ref[...] = gram
+
+        @pl.when(core_ref[0] >= 0)
+        def _():
+            low, piv = eliminate(factored_ref[...])
+            lower_ref[...] = low
+            pivots_ref[...] = piv
+
+        return lower_ref[...], pivots_ref[...]
+
     half = near_ref.shape[0]
     for place, ref in ((core_ref[0], near_ref), (1 - core_ref[0], far_ref)):
         sums_ref[pl.ds(pl.multiple_of(place * half, 8), half), :] = ref[...]
@@ -175,18 +190,18 @@
     x = whole[:RANK, :]
     first = tuple(part[:RANK, :] for part in g)
     h1 = mm_nt(first, first)
-    low1, piv1 = eliminate(h1)
+    low1, piv1 = apart(h1)
     x = turned(low1, piv1, x)
     x = mm(x, g)
     part = split(x)
     h2 = mm_nt(part, part)
-    low2, piv2 = eliminate(h2)
+    low2, piv2 = apart(h2)
     x = turned(low2, piv2, x)
     x = mm(x, g)
     x = mm(x, g)
     y = mm(x, g)
     h3 = mm_nt(x, y)
-    low3, piv3 = eliminate(h3)
+    low3, piv3 = apart(h3)
     turn_t_ref[...] = turned(low3, piv3, x)
     back_ref[...] = turned(low3, piv3, y)
     fine = (smallest(piv1, h1) > 3e-5) & (smallest(piv2, h2) > 1e-4) & (smallest(piv3, h3) > 5e-5)
@@ -236,7 +251,8 @@
             pltpu.VMEM((ORDER, ORDER), f32),
             pltpu.VMEM((RANK, ORDER), f32),
             pltpu.VMEM((RANK, ORDER), f32),
-        ],
+        ]
+        + [pltpu.VMEM((RANK, RANK), f32)] * 3,
         compiler_params=pltpu.CompilerParams(vmem_limit_bytes=32 * 2**20),
     )(here, near, far, wide, weights, place)
 

time: 85.5 us -> 84.8 us (level)
  no operation moved by 1% of the time
where the time goes in v6:
time: 84.8 us; the launch traced here: 84.4 us
  blocking collectives  51.2 us (60%)
  Pallas kernels  19.5 us (23%)
  starting transfers between devices  6.99 us (8%)
  waiting for transfers between devices  5.94 us (7%)
    all_to_all x1, blocking collectives, per_device(): lax.all_to_all(column.reshape(n_item, slab_blocks, width), ITEM, 0, 0, ti...  23.1 us
    all_to_all x2, blocking collectives, copies(): return lax.all_to_all(x, axes, split_axis=0, concat_axis=0, tiled=True)  19.6 us
    pallas_call x1, Pallas kernels, core(): pl.pallas_call(functools.partial(core_kernel, items), out_shape=[jax.Shap...  16.8 us
    all_to_all x1, blocking collectives, summed(): lax.all_to_all(parts, ('item_2', 'item_1'), 0, 0, tiled=True)  8.55 us
    ppermute x3, waiting for transfers between devices, around(): lax.ppermute(x, axis, [(i, (i + k) % n) for i in range(n)])  5.21 us
    ppermute x3, starting transfers between devices, around(): lax.ppermute(x, axis, [(i, (i + k) % n) for i in range(n)])  3.77 us
    ppermute x1, starting transfers between devices, summed(): return (half, lax.ppermute(half, 'item_2', [(0, 1), (1, 0)]))  3.21 us
    pallas_call x1, Pallas kernels, column_of(): pl.pallas_call(column_kernel, out_shape=jax.ShapeDtypeStruct((count, tile...  1.8 us
  transfers between devices with their start and end apart: 4, of which 4 were waited for; matrix products, arithmetic and copies ran while one was open for 0% of the time, Pallas kernels for 0%

profile of v6, /device:TPU:1, one launch (start us, length us, event | category | flops | bytes accessed | tf_op | source)
XLA Modules:
  0.0 84.4 jit_solution(6496814654688141691)
XLA Ops:
  0.6 0.0 copy-start
  0.7 1.8 %shard_map.68 = bf16[256,128]{1,0:T(8,128)(2,1)} custom-call(s32[1]{0:T(128)} %bitcast.2.row_ref, s32[1,256]{1,0:T(1,128)} %bitcast.17, s32[64,256]{1,0:T(8,128)} %bitcast.21, bf16[64,128]{1,0:T(8,128)(2,1)} %bitcast.22), custom_call_target="tpu_custom_call" | custom-call | tf_op jit(solution)/shard_map/pallas_call | solution.py:272
  2.5 23.1 %all_to_all.20 = bf16[64,4,128]{2,1,0:T(4,128)(2,1)S(1)} all-to-all(bf16[64,4,128]{2,1,0:T(4,128)(2,1)} %bitcast.20), channel_id=1, replica_groups=mesh['item_0'=8,'item_1'=4,'item_2'=2,'user'=4] {'item_0','item_1','item..., dimensions={0} | all-to-all | bytes 131072 | tf_op jit(solution)/shard_map/all_to_all | solution.py:393
  25.5 2.7 %collective-permute-start.2 = (bf16[256,128]{1,0:T(8,128)(2,1)S(1)}, bf16[256,128]{1,0:T(8,128)(2,1)S(1)}, u32[]{:S(2)}, u32[]{:S(2)}) collective-permute-start(bf16[256,128]{1,0:T(8,128)(2,1)S(1)} %bitcast.12), channel_id=1, source_target_pairs={{0,3},{1,0},{2,1},{3,2},{4,7},{5,4},{6,5},{7,6},{8,11},{9,8},{10,9... | collective-permute-start | bytes 196616 | tf_op jit(solution)/shard_map/ppermute | solution.py:371
  28.3 0.3 collective-permute-start.1
  28.6 0.7 collective-permute-start
  29.3 0.3 collective-permute-done.2.x3_ref
  29.6 3.4 %collective-permute-done.1.x2_ref = bf16[256,128]{1,0:T(8,128)(2,1)S(1)} collective-permute-done((bf16[256,128]{1,0:T(8,128)(2,1)S(1)}, bf16[256,128]{1,0:T(8,128)(2,1)S(1)}, u32[]{:S(2)}, u32[]{:S(2)}) %collective-permute-start.1) | collective-permute-done | bytes 65568 | tf_op jit(solution)/shard_map/ppermute | solution.py:371
  32.9 1.6 %collective-permute-done.x1_ref = bf16[256,128]{1,0:T(8,128)(2,1)S(1)} collective-permute-done((bf16[256,128]{1,0:T(8,128)(2,1)S(1)}, bf16[256,128]{1,0:T(8,128)(2,1)S(1)}, u32[]{:S(2)}, u32[]{:S(2)}) %collective-permute-start) | collective-permute-done | bytes 65568 | tf_op jit(solution)/shard_map/ppermute | solution.py:371
  34.5 0.0 copy-done
  34.5 0.6 shard_map.69
  35.1 8.5 %all_to_all.21 = f32[8,24,128]{2,1,0:T(8,128)S(1)} all-to-all(f32[8,24,128]{2,1,0:T(8,128)S(1)} %shard_map.69), channel_id=1, replica_groups=mesh['item_0'=8,'item_1'=4,'item_2'=2,'user'=4] {'item_2','item_1'}, dimensions={0} | all-to-all | bytes 196608 | tf_op jit(solution)/shard_map/all_to_all | solution.py:380
  43.7 9.9 %all_to_all.22 = f32[8,24,128]{2,1,0:T(8,128)S(1)} all-to-all(f32[8,24,128]{2,1,0:T(8,128)S(1)} %broadcast_in_dim.6), channel_id=1, replica_groups=mesh['item_0'=8,'item_1'=4,'item_2'=2,'user'=4] {'item_0'}, dimensions={0} | all-to-all | bytes 196608 | tf_op jit(solution)/shard_map/all_to_all | solution.py:376
  53.7 9.7 %all_to_all.23 = f32[16,24,128]{2,1,0:T(8,128)S(1)} all-to-all(f32[16,24,128]{2,1,0:T(8,128)S(1)} %broadcast_in_dim.7), channel_id=1, replica_groups=mesh['item_0'=8,'item_1'=4,'item_2'=2,'user'=4] {'item_1','user'}, dimensions={0} | all-to-all | bytes 393216 | tf_op jit(solution)/shard_map/all_to_all | solution.py:376
  63.3 0.0 copy-start.1
  63.3 0.0 copy-start.2
  63.3 3.2 %collective-permute-start.3 = (f32[384,128]{1,0:T(8,128)S(1)}, f32[384,128]{1,0:T(8,128)S(1)}, u32[]{:S(2)}, u32[]{:S(2)}) collective-permute-start(f32[384,128]{1,0:T(8,128)S(1)} %bitcast.10), channel_id=1, source_target_pairs={{0,4},{4,0},{1,5},{5,1},{2,6},{6,2},{3,7},{7,3},{8,12},{12,8},{9,1... | collective-permute-start | bytes 589832 | tf_op jit(solution)/shard_map/ppermute | solution.py:383
  66.6 0.0 copy-done.1
  66.6 0.0 copy-done.2
  66.6 0.3 shard_map.70
  66.9 0.7 collective-permute-done.3.far_ref
  67.6 16.8 %shard_map.71 = (f32[512,128]{1,0:T(8,128)}, f32[256,128]{1,0:T(8,128)}) custom-call(s32[1]{0:T(128)} %bitcast.core_ref, f32[384,128]{1,0:T(8,128)S(1)} %bitcast.11, f32[384,128]{1,0:T(8,128)S(1)} %collective-permute-done.3.far_ref, bf16[512,640]{1,0:T(8,128)(2,1)S(1)} %get-tuple-element.5.wide_ref, f32[1,128]{1,0:T(1,128)S(1)} %get-tuple-element.6.weights_ref, ...), custom_call_target="tpu_custom_call" | custom-call | tf_op jit(solution)/shard_map/pallas_call | solution.py:245
  (4 shorter events, 0.0 us)
Async XLA Ops:
  0.6 33.9 %copy-start = (f32[512,128]{1,0:T(8,128)S(1)}, f32[512,128]{1,0:T(8,128)}, u32[]{:S(2)}) copy-start(f32[512,128]{1,0:T(8,128)} %basis_ref.3) | copy-start | bytes 786436
  25.5 4.1 %collective-permute-start.2 = (bf16[256,128]{1,0:T(8,128)(2,1)S(1)}, bf16[256,128]{1,0:T(8,128)(2,1)S(1)}, u32[]{:S(2)}, u32[]{:S(2)}) collective-permute-start(bf16[256,128]{1,0:T(8,128)(2,1)S(1)} %bitcast.12), channel_id=1, source_target_pairs={{0,3},{1,0},{2,1},{3,2},{4,7},{5,4},{6,5},{7,6},{8,11},{9,8},{10,9... | collective-permute-start | bytes 196616 | tf_op jit(solution)/shard_map/ppermute | solution.py:371
  28.3 4.7 %collective-permute-start.1 = (bf16[256,128]{1,0:T(8,128)(2,1)S(1)}, bf16[256,128]{1,0:T(8,128)(2,1)S(1)}, u32[]{:S(2)}, u32[]{:S(2)}) collective-permute-start(bf16[256,128]{1,0:T(8,128)(2,1)S(1)} %bitcast.13), channel_id=1, source_target_pairs={{0,2},{1,3},{2,0},{3,1},{4,6},{5,7},{6,4},{7,5},{8,10},{9,11},{10,... | collective-permute-start | bytes 196616 | tf_op jit(solution)/shard_map/ppermute | solution.py:371
  28.6 5.9 %collective-permute-start = (bf16[256,128]{1,0:T(8,128)(2,1)S(1)}, bf16[256,128]{1,0:T(8,128)(2,1)S(1)}, u32[]{:S(2)}, u32[]{:S(2)}) collective-permute-start(bf16[256,128]{1,0:T(8,128)(2,1)S(1)} %bitcast.14), channel_id=1, source_target_pairs={{0,1},{1,2},{2,3},{3,0},{4,5},{5,6},{6,7},{7,4},{8,9},{9,10},{10,1... | collective-permute-start | bytes 196616 | tf_op jit(solution)/shard_map/ppermute | solution.py:371
  63.3 3.2 %copy-start.1 = (s32[256]{0:T(256)S(1)}, s32[256]{0:T(256)}, u32[]{:S(2)}) copy-start(s32[256]{0:T(256)} %param.9) | copy-start | bytes 3076
  63.3 3.2 %copy-start.2 = (f32[128]{0:T(128)S(1)}, f32[128]{0:T(128)}, u32[]{:S(2)}) copy-start(f32[128]{0:T(128)} %param.6) | copy-start | bytes 1540
  63.3 4.3 %collective-permute-start.3 = (f32[384,128]{1,0:T(8,128)S(1)}, f32[384,128]{1,0:T(8,128)S(1)}, u32[]{:S(2)}, u32[]{:S(2)}) collective-permute-start(f32[384,128]{1,0:T(8,128)S(1)} %bitcast.10), channel_id=1, source_target_pairs={{0,4},{4,0},{1,5},{5,1},{2,6},{6,2},{3,7},{7,3},{8,12},{12,8},{9,1... | collective-permute-start | bytes 589832 | tf_op jit(solution)/shard_map/ppermute | solution.py:383

commit v7 on v6

--- a/solution.py
+++ b/solution.py
@@ -132,7 +132,8 @@
 def smallest(pivots, gram):
     i, k = square_iotas()
     start = jnp.sum(jnp.where(i == k, gram, 0.0), axis=1, keepdims=True)
-    return jnp.min(pivots / start)
+    ratio = pivots / start
+    return jnp.min(jnp.where((ratio > 0.0) & (ratio < 2.0), ratio, 0.0))
 
 
 def polished(x, y):

time: 84.8 us -> 84.8 us (level)
  no operation moved by 1% of the time
where the time goes in v7:
time: 84.8 us; the launch traced here: 84.5 us
  blocking collectives  51.2 us (60%)
  Pallas kernels  19.6 us (23%)
  starting transfers between devices  6.99 us (8%)
  waiting for transfers between devices  5.94 us (7%)
    all_to_all x1, blocking collectives, per_device(): lax.all_to_all(column.reshape(n_item, slab_blocks, width), ITEM, 0, 0, ti...  23.1 us
    all_to_all x2, blocking collectives, copies(): return lax.all_to_all(x, axes, split_axis=0, concat_axis=0, tiled=True)  19.6 us
    pallas_call x1, Pallas kernels, core(): pl.pallas_call(functools.partial(core_kernel, items), out_shape=[jax.Shap...  16.8 us
    all_to_all x1, blocking collectives, summed(): lax.all_to_all(parts, ('item_2', 'item_1'), 0, 0, tiled=True)  8.55 us
    ppermute x3, waiting for transfers between devices, around(): lax.ppermute(x, axis, [(i, (i + k) % n) for i in range(n)])  5.21 us
    ppermute x3, starting transfers between devices, around(): lax.ppermute(x, axis, [(i, (i + k) % n) for i in range(n)])  3.77 us
    ppermute x1, starting transfers between devices, summed(): return (half, lax.ppermute(half, 'item_2', [(0, 1), (1, 0)]))  3.21 us
    pallas_call x1, Pallas kernels, column_of(): pl.pallas_call(column_kernel, out_shape=jax.ShapeDtypeStruct((count, tile...  1.8 us
  transfers between devices with their start and end apart: 4, of which 4 were waited for; matrix products, arithmetic and copies ran while one was open for 0% of the time, Pallas kernels for 0%

profile of v7, /device:TPU:1, one launch (start us, length us, event | category | flops | bytes accessed | tf_op | source)
XLA Modules:
  0.0 84.5 jit_solution(11904638433474805719)
XLA Ops:
  0.6 0.0 copy-start
  0.7 1.8 %shard_map.68 = bf16[256,128]{1,0:T(8,128)(2,1)} custom-call(s32[1]{0:T(128)} %bitcast.2.row_ref, s32[1,256]{1,0:T(1,128)} %bitcast.17, s32[64,256]{1,0:T(8,128)} %bitcast.21, bf16[64,128]{1,0:T(8,128)(2,1)} %bitcast.22), custom_call_target="tpu_custom_call" | custom-call | tf_op jit(solution)/shard_map/pallas_call | solution.py:273
  2.5 23.1 %all_to_all.20 = bf16[64,4,128]{2,1,0:T(4,128)(2,1)S(1)} all-to-all(bf16[64,4,128]{2,1,0:T(4,128)(2,1)} %bitcast.20), channel_id=1, replica_groups=mesh['item_0'=8,'item_1'=4,'item_2'=2,'user'=4] {'item_0','item_1','item..., dimensions={0} | all-to-all | bytes 131072 | tf_op jit(solution)/shard_map/all_to_all | solution.py:394
  25.5 2.7 %collective-permute-start.2 = (bf16[256,128]{1,0:T(8,128)(2,1)S(1)}, bf16[256,128]{1,0:T(8,128)(2,1)S(1)}, u32[]{:S(2)}, u32[]{:S(2)}) collective-permute-start(bf16[256,128]{1,0:T(8,128)(2,1)S(1)} %bitcast.12), channel_id=1, source_target_pairs={{0,3},{1,0},{2,1},{3,2},{4,7},{5,4},{6,5},{7,6},{8,11},{9,8},{10,9... | collective-permute-start | bytes 196616 | tf_op jit(solution)/shard_map/ppermute | solution.py:372
  28.3 0.3 collective-permute-start.1
  28.6 0.7 collective-permute-start
  29.3 0.3 collective-permute-done.2.x3_ref
  29.6 3.4 %collective-permute-done.1.x2_ref = bf16[256,128]{1,0:T(8,128)(2,1)S(1)} collective-permute-done((bf16[256,128]{1,0:T(8,128)(2,1)S(1)}, bf16[256,128]{1,0:T(8,128)(2,1)S(1)}, u32[]{:S(2)}, u32[]{:S(2)}) %collective-permute-start.1) | collective-permute-done | bytes 65568 | tf_op jit(solution)/shard_map/ppermute | solution.py:372
  32.9 1.6 %collective-permute-done.x1_ref = bf16[256,128]{1,0:T(8,128)(2,1)S(1)} collective-permute-done((bf16[256,128]{1,0:T(8,128)(2,1)S(1)}, bf16[256,128]{1,0:T(8,128)(2,1)S(1)}, u32[]{:S(2)}, u32[]{:S(2)}) %collective-permute-start) | collective-permute-done | bytes 65568 | tf_op jit(solution)/shard_map/ppermute | solution.py:372
  34.5 0.0 copy-done
  34.5 0.6 shard_map.69
  35.1 8.5 %all_to_all.21 = f32[8,24,128]{2,1,0:T(8,128)S(1)} all-to-all(f32[8,24,128]{2,1,0:T(8,128)S(1)} %shard_map.69), channel_id=1, replica_groups=mesh['item_0'=8,'item_1'=4,'item_2'=2,'user'=4] {'item_2','item_1'}, dimensions={0} | all-to-all | bytes 196608 | tf_op jit(solution)/shard_map/all_to_all | solution.py:381
  43.7 9.9 %all_to_all.22 = f32[8,24,128]{2,1,0:T(8,128)S(1)} all-to-all(f32[8,24,128]{2,1,0:T(8,128)S(1)} %broadcast_in_dim.6), channel_id=1, replica_groups=mesh['item_0'=8,'item_1'=4,'item_2'=2,'user'=4] {'item_0'}, dimensions={0} | all-to-all | bytes 196608 | tf_op jit(solution)/shard_map/all_to_all | solution.py:377
  53.7 9.7 %all_to_all.23 = f32[16,24,128]{2,1,0:T(8,128)S(1)} all-to-all(f32[16,24,128]{2,1,0:T(8,128)S(1)} %broadcast_in_dim.7), channel_id=1, replica_groups=mesh['item_0'=8,'item_1'=4,'item_2'=2,'user'=4] {'item_1','user'}, dimensions={0} | all-to-all | bytes 393216 | tf_op jit(solution)/shard_map/all_to_all | solution.py:377
  63.3 0.0 copy-start.1
  63.3 0.0 copy-start.2
  63.3 3.2 %collective-permute-start.3 = (f32[384,128]{1,0:T(8,128)S(1)}, f32[384,128]{1,0:T(8,128)S(1)}, u32[]{:S(2)}, u32[]{:S(2)}) collective-permute-start(f32[384,128]{1,0:T(8,128)S(1)} %bitcast.10), channel_id=1, source_target_pairs={{0,4},{4,0},{1,5},{5,1},{2,6},{6,2},{3,7},{7,3},{8,12},{12,8},{9,1... | collective-permute-start | bytes 589832 | tf_op jit(solution)/shard_map/ppermute | solution.py:384
  66.6 0.0 copy-done.1
  66.6 0.0 copy-done.2
  66.6 0.3 shard_map.70
  66.9 0.7 collective-permute-done.3.far_ref
  67.6 16.8 %shard_map.71 = (f32[512,128]{1,0:T(8,128)}, f32[256,128]{1,0:T(8,128)}) custom-call(s32[1]{0:T(128)} %bitcast.core_ref, f32[384,128]{1,0:T(8,128)S(1)} %bitcast.11, f32[384,128]{1,0:T(8,128)S(1)} %collective-permute-done.3.far_ref, bf16[512,640]{1,0:T(8,128)(2,1)S(1)} %get-tuple-element.5.wide_ref, f32[1,128]{1,0:T(1,128)S(1)} %get-tuple-element.6.weights_ref, ...), custom_call_target="tpu_custom_call" | custom-call | tf_op jit(solution)/shard_map/pallas_call | solution.py:246
  (4 shorter events, 0.0 us)
Async XLA Ops:
  0.6 33.9 %copy-start = (f32[512,128]{1,0:T(8,128)S(1)}, f32[512,128]{1,0:T(8,128)}, u32[]{:S(2)}) copy-start(f32[512,128]{1,0:T(8,128)} %basis_ref.3) | copy-start | bytes 786436
  25.5 4.1 %collective-permute-start.2 = (bf16[256,128]{1,0:T(8,128)(2,1)S(1)}, bf16[256,128]{1,0:T(8,128)(2,1)S(1)}, u32[]{:S(2)}, u32[]{:S(2)}) collective-permute-start(bf16[256,128]{1,0:T(8,128)(2,1)S(1)} %bitcast.12), channel_id=1, source_target_pairs={{0,3},{1,0},{2,1},{3,2},{4,7},{5,4},{6,5},{7,6},{8,11},{9,8},{10,9... | collective-permute-start | bytes 196616 | tf_op jit(solution)/shard_map/ppermute | solution.py:372
  28.3 4.7 %collective-permute-start.1 = (bf16[256,128]{1,0:T(8,128)(2,1)S(1)}, bf16[256,128]{1,0:T(8,128)(2,1)S(1)}, u32[]{:S(2)}, u32[]{:S(2)}) collective-permute-start(bf16[256,128]{1,0:T(8,128)(2,1)S(1)} %bitcast.13), channel_id=1, source_target_pairs={{0,2},{1,3},{2,0},{3,1},{4,6},{5,7},{6,4},{7,5},{8,10},{9,11},{10,... | collective-permute-start | bytes 196616 | tf_op jit(solution)/shard_map/ppermute | solution.py:372
  28.6 5.9 %collective-permute-start = (bf16[256,128]{1,0:T(8,128)(2,1)S(1)}, bf16[256,128]{1,0:T(8,128)(2,1)S(1)}, u32[]{:S(2)}, u32[]{:S(2)}) collective-permute-start(bf16[256,128]{1,0:T(8,128)(2,1)S(1)} %bitcast.14), channel_id=1, source_target_pairs={{0,1},{1,2},{2,3},{3,0},{4,5},{5,6},{6,7},{7,4},{8,9},{9,10},{10,1... | collective-permute-start | bytes 196616 | tf_op jit(solution)/shard_map/ppermute | solution.py:372
  63.3 3.2 %copy-start.1 = (s32[256]{0:T(256)S(1)}, s32[256]{0:T(256)}, u32[]{:S(2)}) copy-start(s32[256]{0:T(256)} %param.9) | copy-start | bytes 3076
  63.3 3.2 %copy-start.2 = (f32[128]{0:T(128)S(1)}, f32[128]{0:T(128)}, u32[]{:S(2)}) copy-start(f32[128]{0:T(128)} %param.6) | copy-start | bytes 1540
  63.3 4.3 %collective-permute-start.3 = (f32[384,128]{1,0:T(8,128)S(1)}, f32[384,128]{1,0:T(8,128)S(1)}, u32[]{:S(2)}, u32[]{:S(2)}) collective-permute-start(f32[384,128]{1,0:T(8,128)S(1)} %bitcast.10), channel_id=1, source_target_pairs={{0,4},{4,0},{1,5},{5,1},{2,6},{6,2},{3,7},{7,3},{8,12},{12,8},{9,1... | collective-permute-start | bytes 589832 | tf_op jit(solution)/shard_map/ppermute | solution.py:384
